TPU v7x, 512 devices: a whole 4x4x16 slice. The times are simulated.
512 devices in a mesh: replica: 16 (over z), outer: 32 (over x, y, core).
Axes of the slice: x: 4, y: 4, z: 16, core: 2. Of those that a mesh axis runs over, the one named last changes fastest.
Arguments:
- activations: bfloat16 [65536, 4096], P(('replica', 'outer')), may hold values from -6 to 6
- grad_hidden: bfloat16 [65536, 112], P(('replica', 'outer')), may hold values from -0.125 to 0.125
- labels: int32 [65536], P(('replica', 'outer')), may hold values from -100 to 128255, as said below
- lengths: int32 [512, 8], P(('replica', 'outer')), may hold values from 1 to 64, 128 in all within a row
- error_state: float32 [512, 2, 56, 4096], P(('replica', 'outer')), may hold values from -1.5 to 1.5
- warm_start: float32 [2, 8, 4096], replicated, may hold values from -6 to 6
Outputs:
- left_factor: float32 [2, 56, 8], replicated
- right_factor: float32 [2, 8, 4096], replicated
- new_error: float32 [512, 2, 56, 4096], P(('replica', 'outer'))
Inputs may be any that keep to these rules, and one draw needn't show every extreme that they name: `labels`: -100 marks a token without a target; other values are token ids. Every token of the first worker has a target.
All inputs are finite; a program needn't handle non-finite values.
Results may differ from a plain program's by a relative error of at most 0.0095.
Values sent between devices are 32-bit elements; how exact they have to be, the bound alone decides.
No kernel may reach another device: no remote copies, remote signals or barrier semaphores. Data moves between devices by JAX's collectives and lax.ppermute only.
A program may use at most 64 MiB of HBM per device.

v0:
```python
import jax
import jax.numpy as jnp
from jax import lax
from jax.sharding import PartitionSpec as P


def token_mask(labels, lengths_row):
    places = jnp.arange(labels.shape[0], dtype=jnp.int32)
    finals = jnp.cumsum(lengths_row) - 1
    at_final = jnp.any(places[:, None] == finals[None, :], axis=1)
    return jnp.logical_and(labels != -100, jnp.logical_not(at_final))


def orthonormal(p_sum):
    basis = []
    for column in range(p_sum.shape[2]):
        vector = p_sum[:, :, column]
        for earlier in basis:
            vector = vector - jnp.sum(earlier * vector, axis=1, keepdims=True) * earlier
        vector = vector / (jnp.sqrt(jnp.sum(vector * vector, axis=1, keepdims=True)) + 1e-08)
        basis.append(vector)
    return jnp.stack(basis, axis=2)


def project(matrix, warm_start):
    return jnp.einsum("ghc,grc->ghr", matrix, warm_start, precision=lax.Precision.HIGHEST)


def factor_sum(terms):
    return lax.psum(terms, ("replica", "outer"))


def local(activations, grad_hidden, labels, lengths, error_state, warm_start):
    valid_mask = token_mask(labels, lengths[0])
    local_count = jnp.sum(valid_mask.astype(jnp.float32))
    masked = jnp.where(valid_mask[:, None], grad_hidden, jnp.zeros_like(grad_hidden))
    raw_sum = lax.dot_general(
        masked, activations, (((0,), (0,)), ((), ())), preferred_element_type=jnp.float32
    )
    raw_sum = raw_sum.astype(jnp.bfloat16)
    matrices = warm_start.shape[0]
    hidden = error_state.shape[2]
    features = activations.shape[1]
    raw_full = raw_sum.astype(jnp.float32).reshape(matrices, hidden, features)
    carried = error_state[0]
    workers = lax.axis_size("replica") * lax.axis_size("outer")
    all_tokens = float(activations.shape[0] * workers)
    total_valid = lax.psum(local_count, ("replica", "outer"))
    factor = all_tokens / total_valid
    merged = factor * raw_full + carried
    p_sum = factor_sum(project(merged, warm_start))
    left_factor = orthonormal(p_sum)
    q_local = jnp.einsum("ghc,ghr->grc", merged, left_factor, precision=lax.Precision.HIGHEST)
    right_factor = lax.psum(q_local, ("replica", "outer"))
    approx = jnp.einsum("ghr,grc->ghc", left_factor, right_factor, precision=lax.Precision.HIGHEST)
    new_error = merged - approx / workers
    return (left_factor, right_factor, new_error[None])


def solution(mesh):
    placed = (
        P(("replica", "outer"), None),
        P(("replica", "outer"), None),
        P(("replica", "outer")),
        P(("replica", "outer"), None),
        P(("replica", "outer"), None, None, None),
        P(),
    )
    return jax.shard_map(
        local,
        mesh=mesh,
        in_specs=placed,
        out_specs=(P(), P(), P(("replica", "outer"), None, None, None)),
        check_vma=False,
    )
```

profile of v0, /device:TPU:1, one launch (start us, length us, event | category | flops | bytes accessed | tf_op | source)
XLA Modules:
  0.0 691.4 jit_solution(18038038065094104051)
XLA Ops:
  7.2 0.0 copy-start
  7.2 0.0 copy-start.3
  7.2 0.0 all-reduce.2.cloned.1.call-start
  7.2 0.9 reduce-window.8
  8.2 0.1 fusion.7
  8.3 1.3 convert_reduce_fusion
  9.5 111.0 %psum.21 = f32[]{:T(128)} all-reduce(f32[]{:T(128)} %get-tuple-element.78), channel_id=1, replica_groups=mesh['replica'=16,'outer'=32] {'replica','outer'}, use_global_device_ids=true, to_apply=%region_3.4 | all-reduce | flops 1 | bytes 8 | tf_op jit(solution)/shard_map/psum | solution.py:48
  121.2 0.0 copy-start.1
  121.2 0.0 copy-done
  121.2 1.3 fusion.3
  122.5 0.0 copy-done.3
  122.5 0.2 copy-done.1
  122.7 1.7 fusion.18
  124.5 98.6 %psum.22 = f32[2,56,8]{1,0,2:T(2,128)S(1)} all-reduce(f32[2,56,8]{1,0,2:T(2,128)S(1)} %copy.9), channel_id=1, replica_groups=mesh['replica'=16,'outer'=32] {'replica','outer'}, use_global_device_ids=true, to_apply=%region_4.5 | all-reduce | flops 896 | bytes 7168 | tf_op jit(solution)/shard_map/psum | solution.py:30
  223.1 0.1 fusion.15
  223.2 0.2 fusion.13
  223.4 0.1 constant_dynamic-update-slice_fusion.7
  223.4 0.2 multiply_reduce_fusion.27
  223.6 0.2 fusion.8
  223.9 0.3 multiply_reduce_fusion.6
  224.1 0.3 multiply_reduce_fusion.5
  224.4 0.2 multiply_reduce_fusion.22
  224.6 0.2 multiply_reduce_fusion.4
  224.8 0.2 multiply_reduce_fusion.18
  225.0 0.2 multiply_reduce_fusion.3
  225.3 0.2 multiply_reduce_fusion.13
  225.5 0.2 multiply_reduce_fusion.2
  225.7 0.2 multiply_reduce_fusion.7
  225.9 0.2 multiply_reduce_fusion.1
  226.1 0.2 multiply_reduce_fusion
  226.3 0.1 constant_dynamic-update-slice_fusion.6
  226.4 0.1 constant_dynamic-update-slice_fusion.5
  226.4 0.1 constant_dynamic-update-slice_fusion.4
  226.5 0.1 constant_dynamic-update-slice_fusion.3
  226.6 0.1 constant_dynamic-update-slice_fusion.2
  226.7 0.1 constant_dynamic-update-slice_fusion.1
  226.8 0.1 constant_dynamic-update-slice_fusion
  226.9 0.0 copy-start.4
  226.9 3.3 fusion.17
  230.2 0.0 all-reduce.2.cloned.1.call-update
  230.2 449.1 %all-reduce.2.cloned.1.call-done = f32[2,8,4096]{2,1,0:T(8,128)} async-done(((f32[2,8,4096]{2,1,0:T(8,128)}), f32[2,8,4096]{2,1,0:T(8,128)}) %all-reduce.2.cloned.1.call-update) | async-done | bytes 262160 | tf_op jit(solution)/shard_map/psum | solution.py:54
  679.3 0.0 copy-done.4
  679.3 0.0 copy-start.2
  679.3 4.6 fusion.1
  683.9 0.0 copy-done.2
  683.9 0.7 copy.21
  (11 shorter events, 0.1 us)
Async XLA Ops:
  7.2 114.1 %copy-start = (bf16[128,4096]{1,0:T(8,128)(2,1)S(1)}, bf16[128,4096]{1,0:T(8,128)(2,1)}, u32[]{:S(2)}) copy-start(bf16[128,4096]{1,0:T(8,128)(2,1)} %param.6) | copy-start | bytes 3145732
  7.2 115.3 %copy-start.3 = (f32[2,8,4096]{2,1,0:T(8,128)S(1)}, f32[2,8,4096]{2,1,0:T(8,128)}, u32[]{:S(2)}) copy-start(f32[2,8,4096]{2,1,0:T(8,128)} %param.11) | copy-start | bytes 786436
  7.2 672.1 %all-reduce.2.cloned.1.call-start = ((), (), s32[]{:S(2)}) async-start(), calls=%async_computation | async-start | bytes 524288 | tf_op jit(solution)/shard_map/psum | solution.py:54
  121.2 1.5 copy-start.1
  226.9 452.4 %copy-start.4 = (f32[2,56,8]{1,2,0:T(8,128)}, f32[2,56,8]{1,2,0:T(8,128)S(1)}, u32[]{:S(2)}) copy-start(f32[2,56,8]{1,2,0:T(8,128)S(1)} %copy.12) | copy-start | bytes 10756
  679.3 4.6 copy-start.2
Sparse Core Ops, SparseCore 0:
  230.3 448.9 all-reduce.1
where the time goes:
time: 693 us; the launch traced here: 691 us
  waiting for transfers between devices  449 us (65%)
  blocking collectives  210 us (30%)
  between operations  14.9 us (2%)
  matrix products  10.9 us (2%)
    psum x1, waiting for transfers between devices, local(): right_factor = lax.psum(q_local, ('replica', 'outer'))  449 us
    psum x1, blocking collectives, local(): total_valid = lax.psum(local_count, ('replica', 'outer'))  111 us
    psum x1, blocking collectives, factor_sum(): return lax.psum(terms, ('replica', 'outer'))  98.6 us
  transfers between devices with their start and end apart: 1, of which 1 were waited for; matrix products, arithmetic and copies ran while one was open for 0% of the time, Pallas kernels for 0%

commit v1 on v0

v1 whole, which is shorter than its diff:
```python
import jax
import jax.numpy as jnp
from jax import lax
from jax.sharding import PartitionSpec as P

BOTH = ("replica", "outer")


def token_mask(labels, lengths_row):
    places = jnp.arange(labels.shape[0], dtype=jnp.int32)
    finals = jnp.cumsum(lengths_row) - 1
    at_final = jnp.any(places[:, None] == finals[None, :], axis=1)
    return jnp.logical_and(labels != -100, jnp.logical_not(at_final))


def orthonormal(p_sum):
    basis = []
    for column in range(p_sum.shape[2]):
        vector = p_sum[:, :, column]
        for earlier in basis:
            vector = vector - jnp.sum(earlier * vector, axis=1, keepdims=True) * earlier
        vector = vector / (jnp.sqrt(jnp.sum(vector * vector, axis=1, keepdims=True)) + 1e-08)
        basis.append(vector)
    return jnp.stack(basis, axis=2)


def project(matrix, warm_start):
    return jnp.einsum("ghc,grc->ghr", matrix, warm_start, precision=lax.Precision.HIGHEST)


def exchange(blocks, axis):
    return lax.all_to_all(blocks, axis, 0, 0, tiled=True)


def everyone(block, axis):
    return exchange(jnp.broadcast_to(block[None], (lax.axis_size(axis),) + block.shape), axis)


def local(activations, grad_hidden, labels, lengths, error_state, warm_start):
    matrices, rank, features = warm_start.shape
    hidden = error_state.shape[2]
    valid_mask = token_mask(labels, lengths[0])
    local_count = jnp.sum(valid_mask.astype(jnp.float32))
    masked = jnp.where(valid_mask[:, None], grad_hidden, jnp.zeros_like(grad_hidden))
    raw_sum = lax.dot_general(
        masked, activations, (((0,), (0,)), ((), ())), preferred_element_type=jnp.float32
    )
    raw_sum = raw_sum.astype(jnp.bfloat16)
    raw_full = raw_sum.astype(jnp.float32).reshape(matrices, hidden, features)
    carried = error_state[0]
    workers = lax.axis_size("replica") * lax.axis_size("outer")
    all_tokens = float(activations.shape[0] * workers)
    terms = jnp.stack([project(raw_full, warm_start), project(carried, warm_start)]).reshape(-1, 128)
    count_row = jnp.full((1, 128), local_count, jnp.float32)
    payload = jnp.concatenate([terms, count_row, jnp.zeros((1, 128), jnp.float32)], axis=0)
    for axis in ("outer", "replica"):
        payload = jnp.sum(everyone(payload, axis), axis=0)
    total_valid = payload[terms.shape[0], 0]
    factor = all_tokens / total_valid
    sums = payload[: terms.shape[0]].reshape(2, matrices, hidden, rank)
    left_factor = orthonormal(factor * sums[0] + sums[1])
    merged = factor * raw_full + carried
    q_local = jnp.einsum("ghc,ghr->grc", merged, left_factor, precision=lax.Precision.HIGHEST)
    outer = lax.axis_size("outer")
    blocks = q_local.reshape(matrices * rank, outer, features // outer).transpose(1, 0, 2)
    block = jnp.sum(exchange(blocks, "outer"), axis=0)
    block = jnp.sum(everyone(block, "replica"), axis=0)
    right_factor = everyone(block, "outer").transpose(1, 0, 2).reshape(matrices, rank, features)
    approx = jnp.einsum("ghr,grc->ghc", left_factor, right_factor, precision=lax.Precision.HIGHEST)
    new_error = merged - approx / workers
    return (left_factor, right_factor, new_error[None])


def solution(mesh):
    placed = (
        P(BOTH, None),
        P(BOTH, None),
        P(BOTH),
        P(BOTH, None),
        P(BOTH, None, None, None),
        P(),
    )
    return jax.shard_map(
        local,
        mesh=mesh,
        in_specs=placed,
        out_specs=(P(), P(), P(BOTH, None, None, None)),
        check_vma=False,
    )
```

time: 693 us -> 116 us (0.17)
  waiting for transfers between devices: 449 us -> 0 us
  blocking collectives: 210 us -> 90.5 us
  between operations: 14.9 us -> 1.62 us
    psum x1 -> x0, waiting for transfers between devices: 449 us -> none  [local(): right_factor = lax.psum(q_local, ('replica', 'outer'))]
    psum x2 -> x0, blocking collectives: 210 us -> none  [the longest x1 111 us: local(): total_valid = lax.psum(local_count, ('replica', 'outer'))]
    all_to_all x0 -> x5, blocking collectives: none -> 90.5 us  [exchange(): return lax.all_to_all(blocks, axis, 0, 0, tiled=True)]
  transfers between devices with their start and end apart: 1 -> 0, of which waited for: 1 -> 0; matrix products, arithmetic and copies ran while one was open for 0% -> 0% of each run, Pallas kernels for 0% -> 0%
where the time goes in v1:
time: 116 us
  blocking collectives  90.5 us (78%)
  matrix products  11.5 us (10%)
  other arithmetic  9.07 us (8%)
  local copies, waits for them, and re-layouts  2.88 us (2%)
  between operations  1.62 us (1%)
    all_to_all x5, blocking collectives, exchange(): return lax.all_to_all(blocks, axis, 0, 0, tiled=True)  90.5 us
    dot_general x1, matrix products, local(): jnp.einsum('ghr,grc->ghc', left_factor, right_factor, precision=lax.Preci...  4.56 us
    dot_general x2, matrix products, project(): jnp.einsum('ghc,grc->ghr', matrix, warm_start, precision=lax.Precision.HI...  3.99 us
    mul x1, other arithmetic, local(): merged = factor * raw_full + carried  2.74 us
    dot_general x1, matrix products, local(): jnp.einsum('ghc,ghr->grc', merged, left_factor, precision=lax.Precision.H...  2.56 us

profile of v1, /device:TPU:1, one launch (start us, length us, event | category | flops | bytes accessed | tf_op | source)
XLA Modules:
  0.0 115.5 jit_solution(16594404754629949747)
XLA Ops:
  0.7 0.9 reduce-window.8
  1.6 0.1 fusion.10
  1.7 1.3 %convert_reduce_fusion = (f32[]{:T(128)}, pred[128]{0:T(512)(128)(4,1)S(1)}) fusion(pred[128]{0:T(512)(128)(4,1)S(1)} %fusion.10, s32[128]{0:T(128)} %param.8), kind=kLoop, calls=%fused_computation.123 | loop fusion | flops 639 | bytes 772 | tf_op jit(solution)/shard_map/reduce_sum | solution.py:43
  3.0 0.7 pad.1.clone
  3.7 3.2 %fusion.4 = f32[1,2,56,8]{2,3,1,0:T(8,128)S(1)} fusion(f32[2,8,4096]{2,1,0:T(8,128)} %param.11, f32[1,2,56,4096]{3,2,1,0:T(8,128)} %param.10), kind=kOutput, calls=%fused_computation.9 | convolution fusion | flops 44040192 | bytes 2100736 | tf_op jit(solution)/shard_map/ghc,grc->ghr/dot_general | solution.py:28
  6.9 0.4 convolution_convert_fusion
  7.3 0.8 convolution_bitcast_fusion.1
  8.2 0.1 copy.40
  8.3 0.1 reshape.804
  8.5 18.6 %all_to_all.25 = f32[32,16,128]{2,1,0:T(8,128)S(1)} all-to-all(f32[32,16,128]{2,1,0:T(8,128)S(1)} %broadcast_in_dim.28), channel_id=1, replica_groups=mesh['replica'=16,'outer'=32] {'outer'}, dimensions={0} | all-to-all | bytes 524288 | tf_op jit(solution)/shard_map/all_to_all | solution.py:32
  27.2 25.6 %all_to_all.26 = f32[16,16,128]{2,1,0:T(8,128)S(1)} all-to-all(f32[16,16,128]{2,1,0:T(8,128)S(1)} %broadcast_in_dim.29), channel_id=1, replica_groups=mesh['replica'=16,'outer'=32] {'replica'}, dimensions={0} | all-to-all | bytes 262144 | tf_op jit(solution)/shard_map/all_to_all | solution.py:32
  52.8 0.5 slice.49
  54.1 2.7 %convert_multiply_fusion = f32[112,4096]{1,0:T(8,128)} fusion(bf16[112,4096]{1,0:T(8,128)(2,1)} %copy-done.2, f32[]{:T(128)} %bitcast.6), kind=kLoop, calls=%fused_computation.7 | loop fusion | flops 917504 | bytes 2752516 | tf_op jit(solution)/shard_map/mul | solution.py:62
  56.9 0.2 fusion.20
  57.2 0.1 copy.60
  57.3 0.1 copy.59
  57.4 0.1 copy.58
  57.5 0.1 copy.57
  57.6 0.1 copy.54
  57.6 0.1 fusion.18
  57.8 0.1 copy.61
  57.9 0.3 fusion.11
  58.3 0.2 multiply_reduce_fusion.27
  58.5 0.3 multiply_reduce_fusion.6
  58.7 0.2 multiply_reduce_fusion.25
  58.9 0.3 multiply_reduce_fusion.5
  59.2 0.2 multiply_reduce_fusion.22
  59.4 0.2 multiply_reduce_fusion.4
  59.6 0.2 multiply_reduce_fusion.18
  59.8 0.2 multiply_reduce_fusion.3
  60.1 0.2 multiply_reduce_fusion.13
  60.3 0.2 multiply_reduce_fusion.2
  60.5 0.2 multiply_reduce_fusion.7
  60.7 0.2 multiply_reduce_fusion.1
  60.9 0.2 multiply_reduce_fusion
  61.1 0.1 constant_dynamic-update-slice_fusion.6
  61.2 0.1 constant_dynamic-update-slice_fusion.4
  61.3 0.1 constant_dynamic-update-slice_fusion.3
  61.4 0.1 constant_dynamic-update-slice_fusion.2
  61.5 0.1 constant_dynamic-update-slice_fusion.1
  61.6 0.1 constant_dynamic-update-slice_fusion
  61.7 2.6 %convolution_bitcast_fusion = f32[2,8,32,128]{3,1,2,0:T(8,128)S(1)} fusion(f32[2,56,8]{1,2,0:T(8,128)S(1)} %copy.53, f32[2,56,4096]{2,1,0:T(8,128)} %bitcast.92, f32[1,2,56,4096]{3,2,1,0:T(8,128)S(1)} %copy-done.1), kind=kOutput, calls=%fused_computation.8 | convolution fusion | flops 44498944 | bytes 3935744 | tf_op jit(solution)/shard_map/ghc,ghr->grc/dot_general | solution.py:63
  64.3 0.2 copy.64
  64.5 15.1 %all_to_all.27 = f32[32,16,128]{2,1,0:T(8,128)S(1)} all-to-all(f32[32,16,128]{2,1,0:T(8,128)S(1)} %bitcast.96), channel_id=1, replica_groups=mesh['replica'=16,'outer'=32] {'outer'}, dimensions={0} | all-to-all | bytes 524288 | tf_op jit(solution)/shard_map/all_to_all | solution.py:32
  79.7 15.9 %all_to_all.28 = f32[16,16,128]{2,1,0:T(8,128)S(1)} all-to-all(f32[16,16,128]{2,1,0:T(8,128)S(1)} %broadcast_in_dim.30), channel_id=1, replica_groups=mesh['replica'=16,'outer'=32] {'replica'}, dimensions={0} | all-to-all | bytes 262144 | tf_op jit(solution)/shard_map/all_to_all | solution.py:32
  95.7 15.1 %all_to_all.29 = f32[32,16,128]{2,1,0:T(8,128)S(1)} all-to-all(f32[32,16,128]{2,1,0:T(8,128)S(1)} %broadcast_in_dim.31), channel_id=1, replica_groups=mesh['replica'=16,'outer'=32] {'outer'}, dimensions={0} | all-to-all | bytes 524288 | tf_op jit(solution)/shard_map/all_to_all | solution.py:32
  110.8 0.1 copy.51
  111.0 4.6 %fusion.1 = f32[1,2,56,4096]{3,2,1,0:T(8,128)} fusion(f32[2,56,8]{1,2,0:T(8,128)S(1)} %copy.53, f32[2,8,4096]{2,1,0:T(8,128)S(1)} %reshape.806, f32[2,56,4096]{2,1,0:T(8,128)} %bitcast.93, f32[1,2,56,4096]{3,2,1,0:T(8,128)S(1)} %copy-done.1), kind=kOutput, calls=%fused_computation.2 | convolution fusion | flops 45416448 | bytes 5770752 | tf_op jit(solution)/shard_map/ghr,grc->ghc/dot_general | solution.py:69
  (43 shorter events, 0.9 us)
Async XLA Ops:
  0.6 6.3 %copy-start = (bf16[128,4096]{1,0:T(8,128)(2,1)S(1)}, bf16[128,4096]{1,0:T(8,128)(2,1)}, u32[]{:S(2)}) copy-start(bf16[128,4096]{1,0:T(8,128)(2,1)} %param.6) | copy-start | bytes 3145732
  0.6 6.3 %copy-start.6 = (bf16[128,112]{0,1:T(8,128)(2,1)S(1)}, bf16[128,112]{0,1:T(8,128)(2,1)}, u32[]{:S(2)}) copy-start(bf16[128,112]{0,1:T(8,128)(2,1)} %param.7) | copy-start | bytes 86020
  3.7 3.6 %copy-start.4 = (f32[2,8,4096]{2,1,0:T(8,128)S(1)}, f32[2,8,4096]{2,1,0:T(8,128)}, u32[]{:S(2)}) copy-start(f32[2,8,4096]{2,1,0:T(8,128)} %param.11) | copy-start | bytes 786436
  7.3 46.7 %copy-start.2 = (bf16[112,4096]{1,0:T(8,128)(2,1)}, bf16[112,4096]{1,0:T(8,128)(2,1)S(1)}, u32[]{:S(2)}) copy-start(bf16[112,4096]{1,0:T(8,128)(2,1)S(1)} %convolution_convert_fusion) | copy-start | bytes 2752516
  54.0 7.6 %copy-start.1 = (f32[1,2,56,4096]{3,2,1,0:T(8,128)S(1)}, f32[1,2,56,4096]{3,2,1,0:T(8,128)}, u32[]{:S(2)}) copy-start(f32[1,2,56,4096]{3,2,1,0:T(8,128)} %param.10) | copy-start | bytes 5505028
  61.7 49.3 %copy-start.5 = (f32[2,56,8]{1,2,0:T(8,128)}, f32[2,56,8]{1,2,0:T(8,128)S(1)}, u32[]{:S(2)}) copy-start(f32[2,56,8]{1,2,0:T(8,128)S(1)} %copy.53) | copy-start | bytes 10756
  111.0 4.6 %copy-start.3 = (f32[2,8,4096]{2,1,0:T(8,128)}, f32[2,8,4096]{2,1,0:T(8,128)S(1)}, u32[]{:S(2)}) copy-start(f32[2,8,4096]{2,1,0:T(8,128)S(1)} %reshape.806) | copy-start | bytes 786436

commit v2 on v1

v2 whole, which is shorter than its diff:
```python
import functools

import jax
import jax.numpy as jnp
from jax import lax
from jax.experimental import pallas as pl
from jax.experimental.pallas import tpu as pltpu
from jax.sharding import PartitionSpec as P

BOTH = ("replica", "outer")
F32, BF16 = jnp.float32, jnp.bfloat16
HALF = 64
TILE = 1024


def halves(x):
    high = x.astype(BF16)
    return high, (x - high.astype(F32)).astype(BF16)


def padded(first, second):
    gap = jnp.zeros((HALF - first.shape[0], first.shape[1]), first.dtype)
    return jnp.concatenate([first, gap, second, gap], axis=0)


def dot(a, b):
    return lax.dot_general(a, b, (((1,), (0,)), ((), ())), preferred_element_type=F32)


def dot_rows(a, b):
    return lax.dot_general(a, b, (((1,), (1,)), ((), ())), preferred_element_type=F32)


def terms_kernel(len_ref, label_ref, grad_ref, act_ref, err_ref, warm_ref, raw_ref, pay_ref, masked_ref):
    hidden = err_ref.shape[2]
    rank = warm_ref.shape[1]
    lane = lax.broadcasted_iota(jnp.int32, (1, 128), 1)

    @pl.when(pl.program_id(0) == 0)
    def _():
        mask = label_ref[...] != -100
        final = -1
        for document in range(len_ref.shape[1]):
            final = final + len_ref[0, document]
            mask = jnp.logical_and(mask, lane != final)
        grad = grad_ref[...].astype(F32)
        grad = padded(grad[:hidden], grad[hidden:])
        masked_ref[...] = jnp.where(mask, grad, 0.0).astype(BF16)
        count = jnp.sum(mask.astype(F32), axis=1, keepdims=True)
        row = lax.broadcasted_iota(jnp.int32, pay_ref.shape, 0)
        at = jnp.logical_and(row == 0, lane == 127)
        pay_ref[...] = jnp.where(at, count, 0.0)

    raw = dot(masked_ref[...], act_ref[...]).astype(BF16)
    raw_ref[...] = raw
    warm = warm_ref[...].reshape(2 * rank, warm_ref.shape[2])
    high = warm.astype(BF16)
    rest = warm - high.astype(F32)
    middle, low = halves(rest)
    split = jnp.concatenate([high, middle, low], axis=0)
    of_raw = dot_rows(split, raw)
    n = 2 * rank
    of_raw = of_raw[:n] + (of_raw[n : 2 * n] + of_raw[2 * n :])
    carried_high, carried_low = halves(padded(err_ref[0, 0], err_ref[0, 1]))
    of_err = dot_rows(split[: 2 * n], carried_high)
    of_err = of_err[:n] + (of_err[n:] + dot_rows(high, carried_low))
    left = lane < HALF
    pay_ref[:rank] += jnp.where(left, of_raw[:rank], of_raw[rank:])
    pay_ref[rank:] += jnp.where(left, of_err[:rank], of_err[rank:])


def basis_of(vectors):
    row = lax.broadcasted_iota(jnp.int32, (vectors.shape[0], 1), 0)
    for r in range(vectors.shape[0]):
        current = vectors[r : r + 1]
        dots = jnp.sum(vectors * current, axis=1, keepdims=True)
        norm = jnp.sqrt(dots[r : r + 1]) + 1e-08
        unit = current / norm
        later = vectors - (dots / norm) * unit
        vectors = jnp.where(row == r, unit, jnp.where(row > r, later, vectors))
    return vectors


def factor_of(pay_ref, all_tokens):
    return all_tokens / pay_ref[0:1, 127:128]


def right_kernel(all_tokens, pay_ref, raw_ref, err_ref, left_ref, basis_ref, q_ref, lhs_ref):
    rank = pay_ref.shape[0] // 2
    hidden = err_ref.shape[2]
    factor = factor_of(pay_ref, all_tokens)

    @pl.when(pl.program_id(0) == 0)
    def _():
        lane = lax.broadcasted_iota(jnp.int32, (1, 128), 1)
        p_sum = factor * pay_ref[:rank] + pay_ref[rank:]
        first = basis_of(jnp.where(lane < hidden, p_sum, 0.0))
        of_second = jnp.logical_and(lane >= HALF, lane < HALF + hidden)
        second = basis_of(jnp.where(of_second, p_sum, 0.0))
        left_ref[0] = first[:, :hidden]
        left_ref[1] = pltpu.roll(second, HALF, 1)[:, :hidden]
        basis = jnp.concatenate([first, second], axis=0)
        basis_ref[...] = basis
        high, low = halves(basis)
        top = jnp.concatenate([high, high], axis=1)
        bottom = jnp.concatenate([low, jnp.zeros_like(low)], axis=1)
        lhs_ref[...] = jnp.concatenate([top, bottom], axis=0)

    merged = factor * raw_ref[...].astype(F32) + padded(err_ref[0, 0], err_ref[0, 1])
    high, low = halves(merged)
    both = dot(lhs_ref[...], jnp.concatenate([high, low], axis=0))
    q_local = both[: 2 * rank] + both[2 * rank :]
    width = q_ref.shape[2]
    for block in range(q_ref.shape[0]):
        q_ref[block] = q_local[:, block * width : (block + 1) * width]


def error_kernel(all_tokens, workers, pay_ref, basis_ref, sum_ref, raw_ref, err_ref, right_ref, new_ref, lhs_ref):
    rank = pay_ref.shape[0] // 2
    hidden = err_ref.shape[2]

    @pl.when(pl.program_id(0) == 0)
    def _():
        high, low = halves(basis_ref[...])
        high, low = high.astype(F32), low.astype(F32)
        gap = jnp.zeros((128 - 6 * rank, 128), F32)
        stacked = jnp.concatenate([high, high, low, gap], axis=0)
        lhs_ref[...] = stacked.T.astype(BF16)

    summed = jnp.concatenate([sum_ref[block] for block in range(sum_ref.shape[0])], axis=1)
    right_ref[0] = summed[:rank]
    right_ref[1] = summed[rank:]
    high, low = halves(summed * (1.0 / workers))
    gap = jnp.zeros((128 - 6 * rank, high.shape[1]), BF16)
    approx = dot(lhs_ref[...], jnp.concatenate([high, low, high, gap], axis=0))
    factor = factor_of(pay_ref, all_tokens)
    for matrix in range(2):
        rows = slice(matrix * HALF, matrix * HALF + HALF)
        raw = raw_ref[rows, :].astype(F32)[:hidden]
        new_ref[0, matrix] = factor * raw + err_ref[0, matrix] - approx[rows][:hidden]


def exchange(blocks, axis):
    return lax.all_to_all(blocks, axis, 0, 0, tiled=True)


def everyone(block, axis):
    return exchange(jnp.broadcast_to(block[None], (lax.axis_size(axis),) + block.shape), axis)


def whole(shape):
    return pl.BlockSpec(shape, lambda i: (0,) * len(shape))


def local(activations, grad_hidden, labels, lengths, error_state, warm_start):
    matrices, rank, features = warm_start.shape
    hidden = error_state.shape[2]
    tokens = activations.shape[0]
    outer = lax.axis_size("outer")
    workers = lax.axis_size("replica") * outer
    all_tokens = float(tokens * workers)
    width = features // outer
    grid = (features // TILE,)
    params = pltpu.CompilerParams(vmem_limit_bytes=24 * 2**20)
    err_spec = pl.BlockSpec((1, matrices, hidden, TILE), lambda i: (0, 0, 0, i))
    raw_spec = pl.BlockSpec((2 * HALF, TILE), lambda i: (0, i))
    warm_spec = pl.BlockSpec((matrices, rank, TILE), lambda i: (0, 0, i))
    block_spec = pl.BlockSpec((TILE // width, 2 * rank, width), lambda i: (i, 0, 0))
    raw, payload = pl.pallas_call(
        terms_kernel,
        grid=grid,
        in_specs=[
            pl.BlockSpec(memory_space=pltpu.SMEM),
            whole((1, tokens)),
            whole((matrices * hidden, tokens)),
            pl.BlockSpec((tokens, TILE), lambda i: (0, i)),
            err_spec,
            warm_spec,
        ],
        out_specs=[raw_spec, whole((2 * rank, 128))],
        out_shape=[
            jax.ShapeDtypeStruct((2 * HALF, features), BF16),
            jax.ShapeDtypeStruct((2 * rank, 128), F32),
        ],
        scratch_shapes=[pltpu.VMEM((2 * HALF, tokens), BF16)],
        compiler_params=params,
        name="terms",
    )(lengths, labels.reshape(1, tokens), grad_hidden.T, activations, error_state, warm_start)
    for axis in ("outer", "replica"):
        payload = jnp.sum(everyone(payload, axis), axis=0)
    left_rows, basis, q_local = pl.pallas_call(
        functools.partial(right_kernel, all_tokens),
        grid=grid,
        in_specs=[whole((2 * rank, 128)), raw_spec, err_spec],
        out_specs=[whole((matrices, rank, hidden)), whole((2 * rank, 128)), block_spec],
        out_shape=[
            jax.ShapeDtypeStruct((matrices, rank, hidden), F32),
            jax.ShapeDtypeStruct((2 * rank, 128), F32),
            jax.ShapeDtypeStruct((outer, 2 * rank, width), F32),
        ],
        scratch_shapes=[pltpu.VMEM((4 * rank, 256), BF16)],
        compiler_params=params,
        name="right",
    )(payload, raw, error_state)
    block = jnp.sum(exchange(q_local, "outer"), axis=0)
    block = jnp.sum(everyone(block, "replica"), axis=0)
    summed = everyone(block, "outer")
    right_factor, new_error = pl.pallas_call(
        functools.partial(error_kernel, all_tokens, workers),
        grid=grid,
        in_specs=[whole((2 * rank, 128)), whole((2 * rank, 128)), block_spec, raw_spec, err_spec],
        out_specs=[warm_spec, err_spec],
        out_shape=[
            jax.ShapeDtypeStruct((matrices, rank, features), F32),
            jax.ShapeDtypeStruct((1, matrices, hidden, features), F32),
        ],
        scratch_shapes=[pltpu.VMEM((2 * HALF, 128), BF16)],
        compiler_params=params,
        name="error",
    )(payload, basis, summed, raw, error_state)
    return (left_rows.transpose(0, 2, 1), right_factor, new_error)


def solution(mesh):
    placed = (
        P(BOTH, None),
        P(BOTH, None),
        P(BOTH),
        P(BOTH, None),
        P(BOTH, None, None, None),
        P(),
    )
    return jax.shard_map(
        local,
        mesh=mesh,
        in_specs=placed,
        out_specs=(P(), P(), P(BOTH, None, None, None)),
        check_vma=False,
    )
```

time: 116 us -> 105 us (0.905)
  matrix products: 11.5 us -> 0 us
  other arithmetic: 9.07 us -> 0.11 us
  Pallas kernels: 0 us -> 7.87 us
  local copies, waits for them, and re-layouts: 2.88 us -> 5.79 us
    dot_general x5 -> x0, matrix products: 11.5 us -> none  [the longest x1 4.56 us: local(): jnp.einsum('ghr,grc->ghc', left_factor, right_factor, precision=lax.Preci...]
    pallas_call x0 -> x3, Pallas kernels: none -> 7.87 us  [the longest x1 2.81 us: local(): pl.pallas_call(functools.partial(right_kernel, all_tokens), grid=grid, in...]
    unnamed x24 -> x14, local copies, waits for them, and re-layouts: 0.77 us -> 5.73 us
    reduce_sum x17 -> x1, other arithmetic: 4.43 us -> 0.04 us  [local(): block = jnp.sum(exchange(q_local, 'outer'), axis=0)]
    mul x1 -> x0, other arithmetic: 2.74 us -> none  [local(): merged = factor * raw_full + carried]
where the time goes in v2:
time: 105 us
  blocking collectives  90.5 us (86%)
  Pallas kernels  7.87 us (7%)
  local copies, waits for them, and re-layouts  5.79 us (6%)
    all_to_all x5, blocking collectives, exchange(): return lax.all_to_all(blocks, axis, 0, 0, tiled=True)  90.5 us
    unnamed x14, local copies, waits for them, and re-layouts  5.73 us
    pallas_call x1, Pallas kernels, local(): pl.pallas_call(functools.partial(right_kernel, all_tokens), grid=grid, in...  2.81 us
    pallas_call x1, Pallas kernels, local(): pl.pallas_call(terms_kernel, grid=grid, in_specs=[pl.BlockSpec(memory_spa...  2.61 us
    pallas_call x1, Pallas kernels, local(): pl.pallas_call(functools.partial(error_kernel, all_tokens, workers), grid...  2.44 us

profile of v2, /device:TPU:1, one launch (start us, length us, event | category | flops | bytes accessed | tf_op | source)
XLA Modules:
  0.0 104.9 jit_solution(17189394049819278050)
XLA Ops:
  0.6 0.0 copy-start
  0.6 1.5 %copy-done = f32[1,2,56,4096]{3,2,1,0:T(8,128)S(1)} copy-done((f32[1,2,56,4096]{3,2,1,0:T(8,128)S(1)}, f32[1,2,56,4096]{3,2,1,0:T(8,128)}, u32[]{:S(2)}) %copy-start) | copy-done | bytes 1835032
  2.1 0.0 copy-start.2
  2.1 1.2 %copy-done.2 = bf16[128,4096]{1,0:T(8,128)(2,1)S(1)} copy-done((bf16[128,4096]{1,0:T(8,128)(2,1)S(1)}, bf16[128,4096]{1,0:T(8,128)(2,1)}, u32[]{:S(2)}) %copy-start.2) | copy-done | bytes 1048600
  3.4 0.0 copy-start.3
  3.4 0.9 copy-done.3
  4.3 0.0 copy-start.4
  4.3 0.7 copy-done.4
  5.1 0.0 copy-start.5
  5.1 0.7 copy-done.5
  5.7 0.0 copy-start.6
  5.7 0.7 copy-done.6
  6.4 0.0 copy-start.1
  6.4 2.6 %terms.1 = (bf16[128,4096]{1,0:T(8,128)(2,1)S(1)}, f32[16,128]{1,0:T(8,128)S(1)}) custom-call(s32[1,8]{1,0:T(1,128)S(1)} %copy-done.5, s32[1,128]{1,0:T(1,128)S(1)} %bitcast.4, bf16[112,128]{1,0:T(8,128)(2,1)S(1)} %bitcast.3, bf16[128,4096]{1,0:T(8,128)(2,1)S(1)} %copy-done.2, f32[1,2,56,4096]{3,2,1,0:T(8,128)S(1)} %copy-done, f32[2,8,4096]{2,1,0:T(8,128)S(1)} %copy-done.3), custom_call_target="tpu_custom_call" | custom-call | tf_op jit(solution)/shard_map/terms/pallas_call | solution.py:169
  9.0 18.6 %all_to_all.25 = f32[32,16,128]{2,1,0:T(8,128)S(1)} all-to-all(f32[32,16,128]{2,1,0:T(8,128)S(1)} %broadcast_in_dim.8), channel_id=1, replica_groups=mesh['replica'=16,'outer'=32] {'outer'}, dimensions={0} | all-to-all | bytes 524288 | tf_op jit(solution)/shard_map/all_to_all | solution.py:144
  27.7 25.6 %all_to_all.26 = f32[16,16,128]{2,1,0:T(8,128)S(1)} all-to-all(f32[16,16,128]{2,1,0:T(8,128)S(1)} %broadcast_in_dim.9), channel_id=1, replica_groups=mesh['replica'=16,'outer'=32] {'replica'}, dimensions={0} | all-to-all | bytes 262144 | tf_op jit(solution)/shard_map/all_to_all | solution.py:144
  53.3 0.0 copy-done.1
  53.4 2.8 %right.1 = (f32[2,8,56]{2,1,0:T(8,128)}, f32[16,128]{1,0:T(8,128)S(1)}, f32[32,16,128]{2,1,0:T(8,128)S(1)}) custom-call(f32[16,128]{1,0:T(8,128)S(1)} %reduce_sum.37.pay_ref, bf16[128,4096]{1,0:T(8,128)(2,1)S(1)} %get-tuple-element.11.raw_ref, f32[1,2,56,4096]{3,2,1,0:T(8,128)S(1)} %copy-done.1), custom_call_target="tpu_custom_call" | custom-call | tf_op jit(solution)/shard_map/right/pallas_call | solution.py:191
  56.2 15.1 %all_to_all.27 = f32[32,16,128]{2,1,0:T(8,128)S(1)} all-to-all(f32[32,16,128]{2,1,0:T(8,128)S(1)} %get-tuple-element.14), channel_id=1, replica_groups=mesh['replica'=16,'outer'=32] {'outer'}, dimensions={0} | all-to-all | bytes 524288 | tf_op jit(solution)/shard_map/all_to_all | solution.py:144
  71.4 15.9 %all_to_all.28 = f32[16,16,128]{2,1,0:T(8,128)S(1)} all-to-all(f32[16,16,128]{2,1,0:T(8,128)S(1)} %broadcast_in_dim.10), channel_id=1, replica_groups=mesh['replica'=16,'outer'=32] {'replica'}, dimensions={0} | all-to-all | bytes 262144 | tf_op jit(solution)/shard_map/all_to_all | solution.py:144
  87.3 15.1 %all_to_all.29.sum_ref = f32[32,16,128]{2,1,0:T(8,128)S(1)} all-to-all(f32[32,16,128]{2,1,0:T(8,128)S(1)} %broadcast_in_dim.11), channel_id=1, replica_groups=mesh['replica'=16,'outer'=32] {'outer'}, dimensions={0} | all-to-all | bytes 524288 | tf_op jit(solution)/shard_map/all_to_all | solution.py:144
  102.5 2.4 %error.1 = (f32[2,8,4096]{2,1,0:T(8,128)}, f32[1,2,56,4096]{3,2,1,0:T(8,128)}) custom-call(f32[16,128]{1,0:T(8,128)S(1)} %reduce_sum.37.pay_ref, f32[16,128]{1,0:T(8,128)S(1)} %get-tuple-element.13.basis_ref, f32[32,16,128]{2,1,0:T(8,128)S(1)} %all_to_all.29.sum_ref, bf16[128,4096]{1,0:T(8,128)(2,1)S(1)} %get-tuple-element.11.raw_ref, ...), custom_call_target="tpu_custom_call" | custom-call | tf_op jit(solution)/shard_map/error/pallas_call | solution.py:208
  (8 shorter events, 0.2 us)
Async XLA Ops:
  0.6 1.5 %copy-start = (f32[1,2,56,4096]{3,2,1,0:T(8,128)S(1)}, f32[1,2,56,4096]{3,2,1,0:T(8,128)}, u32[]{:S(2)}) copy-start(f32[1,2,56,4096]{3,2,1,0:T(8,128)} %err_ref.5) | copy-start | bytes 5505028
  2.1 1.2 %copy-start.2 = (bf16[128,4096]{1,0:T(8,128)(2,1)S(1)}, bf16[128,4096]{1,0:T(8,128)(2,1)}, u32[]{:S(2)}) copy-start(bf16[128,4096]{1,0:T(8,128)(2,1)} %act_ref.1) | copy-start | bytes 3145732
  3.4 0.9 copy-start.3
  4.3 0.7 copy-start.4
  5.1 0.7 copy-start.5
  5.7 0.7 copy-start.6
  6.4 47.0 %copy-start.1 = (f32[1,2,56,4096]{3,2,1,0:T(8,128)S(1)}, f32[1,2,56,4096]{3,2,1,0:T(8,128)}, u32[]{:S(2)}) copy-start(f32[1,2,56,4096]{3,2,1,0:T(8,128)} %err_ref.5) | copy-start | bytes 5505028

commit v3 on v1

v3 whole, which is shorter than its diff:
```python
import functools

import jax
import jax.numpy as jnp
from jax import lax
from jax.experimental import pallas as pl
from jax.experimental.pallas import tpu as pltpu
from jax.sharding import PartitionSpec as P

BOTH = ("replica", "outer")
F32, BF16 = jnp.float32, jnp.bfloat16
HALF = 64
TILE = 1024


def halves(x):
    high = x.astype(BF16)
    return high, (x - high.astype(F32)).astype(BF16)


def padded(first, second):
    gap = jnp.zeros((HALF - first.shape[0], first.shape[1]), first.dtype)
    return jnp.concatenate([first, gap, second, gap], axis=0)


def dot(a, b):
    return lax.dot_general(a, b, (((1,), (0,)), ((), ())), preferred_element_type=F32)


def dot_rows(a, b):
    return lax.dot_general(a, b, (((1,), (1,)), ((), ())), preferred_element_type=F32)


def terms_kernel(len_ref, label_ref, grad_ref, act_ref, err_ref, warm_ref, raw_ref, pay_ref):
    hidden = err_ref.shape[2]
    rank = warm_ref.shape[1]
    n = 2 * rank
    lane = lax.broadcasted_iota(jnp.int32, (1, 128), 1)
    mask = label_ref[...] != -100
    final = -1
    for document in range(len_ref.shape[1]):
        final = final + len_ref[0, document]
        mask = jnp.logical_and(mask, lane != final)
    count = jnp.sum(mask.astype(F32), axis=1, keepdims=True)
    grad = grad_ref[...].astype(F32)
    grad = padded(grad[:hidden], grad[hidden:])
    masked = jnp.where(mask, grad, 0.0).astype(BF16)
    raw = dot(masked, act_ref[...]).astype(BF16)
    raw_ref[...] = raw
    warm = warm_ref[...].reshape(n, warm_ref.shape[2])
    high = warm.astype(BF16)
    middle, low = halves(warm - high.astype(F32))
    split = jnp.concatenate([high, middle, low], axis=0)
    of_raw = dot_rows(split, raw)
    of_raw = of_raw[:n] + (of_raw[n : 2 * n] + of_raw[2 * n :])
    carried_high, carried_low = halves(padded(err_ref[0, 0], err_ref[0, 1]))
    of_err = dot_rows(split[: 2 * n], carried_high)
    of_err = of_err[:n] + (of_err[n:] + dot_rows(high, carried_low))
    left = lane < HALF
    row = lax.broadcasted_iota(jnp.int32, (rank, 128), 0)
    at_count = jnp.logical_and(row == 0, lane == 127)
    pay_ref[:rank] = jnp.where(at_count, count, jnp.where(left, of_raw[:rank], of_raw[rank:]))
    pay_ref[rank:] = jnp.where(left, of_err[:rank], of_err[rank:])


def basis_of(vectors):
    row = lax.broadcasted_iota(jnp.int32, (vectors.shape[0], 1), 0)
    for r in range(vectors.shape[0]):
        current = vectors[r : r + 1]
        dots = jnp.sum(vectors * current, axis=1, keepdims=True)
        norm = jnp.sqrt(dots[r : r + 1]) + 1e-08
        unit = current / norm
        later = vectors - (dots / norm) * unit
        vectors = jnp.where(row == r, unit, jnp.where(row > r, later, vectors))
    return vectors


def factor_of(pay_ref, all_tokens):
    return all_tokens / pay_ref[0:1, 127:128]


def right_kernel(all_tokens, pay_ref, raw_ref, err_ref, left_ref, basis_ref, q_ref):
    rank = pay_ref.shape[0] // 2
    hidden = err_ref.shape[2]
    factor = factor_of(pay_ref, all_tokens)
    lane = lax.broadcasted_iota(jnp.int32, (1, 128), 1)
    p_sum = factor * pay_ref[:rank] + pay_ref[rank:]
    first = basis_of(jnp.where(lane < hidden, p_sum, 0.0))
    of_second = jnp.logical_and(lane >= HALF, lane < HALF + hidden)
    second = basis_of(jnp.where(of_second, p_sum, 0.0))
    left_ref[0] = first[:, :hidden]
    left_ref[1] = pltpu.roll(second, HALF, 1)[:, :hidden]
    basis = jnp.concatenate([first, second], axis=0)
    basis_ref[...] = basis
    high, low = halves(basis)
    top = jnp.concatenate([high, high], axis=1)
    bottom = jnp.concatenate([low, jnp.zeros_like(low)], axis=1)
    lhs = jnp.concatenate([top, bottom], axis=0)
    width = q_ref.shape[2]
    for part in range(raw_ref.shape[1] // TILE):
        at = pl.ds(part * TILE, TILE)
        carried = padded(err_ref[0, 0, :, at], err_ref[0, 1, :, at])
        high, low = halves(factor * raw_ref[:, at].astype(F32) + carried)
        both = dot(lhs, jnp.concatenate([high, low], axis=0))
        q_local = both[: 2 * rank] + both[2 * rank :]
        for block in range(TILE // width):
            q_ref[part * (TILE // width) + block] = q_local[:, block * width : (block + 1) * width]


def error_kernel(
    all_tokens, workers, pay_ref, basis_ref, sum_ref, raw_ref, err_ref, right_hbm, new_hbm,
    right_ref, new_ref, sems,
):
    rank = pay_ref.shape[0] // 2
    hidden = err_ref.shape[2]
    width = sum_ref.shape[2]
    high, low = halves(basis_ref[...])
    high, low = high.astype(F32), low.astype(F32)
    gap = jnp.zeros((128 - 6 * rank, 128), F32)
    lhs = jnp.concatenate([high, high, low, gap], axis=0).T.astype(BF16)
    factor = factor_of(pay_ref, all_tokens)
    copies = []
    for part in range(raw_ref.shape[1] // TILE):
        at = pl.ds(part * TILE, TILE)
        blocks = TILE // width
        summed = jnp.concatenate([sum_ref[part * blocks + block] for block in range(blocks)], axis=1)
        right_ref[0, :, at] = summed[:rank]
        right_ref[1, :, at] = summed[rank:]
        copies.append(pltpu.make_async_copy(right_ref.at[:, :, at], right_hbm.at[:, :, at], sems.at[0, part]))
        copies[-1].start()
        high, low = halves(summed * (1.0 / workers))
        gap = jnp.zeros((128 - 6 * rank, TILE), BF16)
        approx = dot(lhs, jnp.concatenate([high, low, high, gap], axis=0))
        for matrix in range(2):
            rows = slice(matrix * HALF, matrix * HALF + HALF)
            raw = raw_ref[rows, at].astype(F32)[:hidden]
            new_ref[0, matrix, :, at] = factor * raw + err_ref[0, matrix, :, at] - approx[rows][:hidden]
        copies.append(pltpu.make_async_copy(new_ref.at[:, :, :, at], new_hbm.at[:, :, :, at], sems.at[1, part]))
        copies[-1].start()
    for each in copies:
        each.wait()


def exchange(blocks, axis):
    return lax.all_to_all(blocks, axis, 0, 0, tiled=True)


def everyone(block, axis):
    return exchange(jnp.broadcast_to(block[None], (lax.axis_size(axis),) + block.shape), axis)


ANY = pl.BlockSpec(memory_space=pl.ANY)
VMEM = pl.BlockSpec(memory_space=pltpu.VMEM)
LIMIT = 16 * 2**20


def terms(lengths, labels, grad, activations, error_state, warm_start):
    _, rank, features = warm_start.shape
    operands = (labels, grad, activations, error_state, warm_start)
    raw = jax.ShapeDtypeStruct((2 * HALF, features), BF16)
    payload = jax.ShapeDtypeStruct((2 * rank, 128), F32)

    def once(x):
        return pl.BlockSpec(x.shape, lambda i: (0,) * len(x.shape))

    return pl.pallas_call(
        terms_kernel,
        grid=(1,),
        in_specs=[pl.BlockSpec(memory_space=pltpu.SMEM)] + [once(x) for x in operands],
        out_specs=[once(raw), once(payload)],
        out_shape=[raw, payload],
        name="terms",
    )(lengths, *operands)


def right(all_tokens, outer, payload, raw, error_state):
    rank = payload.shape[0] // 2
    hidden, features = error_state.shape[2:]
    return pl.pallas_call(
        functools.partial(right_kernel, all_tokens),
        in_specs=[VMEM] * 3,
        out_specs=[VMEM] * 3,
        out_shape=[
            jax.ShapeDtypeStruct((2, rank, hidden), F32),
            jax.ShapeDtypeStruct((2 * rank, 128), F32),
            jax.ShapeDtypeStruct((outer, 2 * rank, features // outer), F32),
        ],
        compiler_params=pltpu.CompilerParams(vmem_limit_bytes=LIMIT),
        name="right",
    )(payload, raw, error_state)


def error(all_tokens, workers, payload, basis, summed, raw, error_state):
    rank = payload.shape[0] // 2
    features = error_state.shape[3]
    right_factor = jax.ShapeDtypeStruct((2, rank, features), F32)
    return pl.pallas_call(
        functools.partial(error_kernel, all_tokens, workers),
        in_specs=[VMEM] * 5,
        out_specs=[ANY] * 2,
        out_shape=[right_factor, jax.ShapeDtypeStruct(error_state.shape, F32)],
        scratch_shapes=[
            pltpu.VMEM(right_factor.shape, F32),
            pltpu.VMEM(error_state.shape, F32),
            pltpu.SemaphoreType.DMA((2, features // TILE)),
        ],
        compiler_params=pltpu.CompilerParams(vmem_limit_bytes=LIMIT),
        name="error",
    )(payload, basis, summed, raw, error_state)


def local(activations, grad_hidden, labels, lengths, error_state, warm_start):
    outer = lax.axis_size("outer")
    workers = lax.axis_size("replica") * outer
    all_tokens = float(activations.shape[0] * workers)
    raw, payload = terms(
        lengths, labels.reshape(1, -1), grad_hidden.T, activations, error_state, warm_start
    )
    for axis in ("outer", "replica"):
        payload = jnp.sum(everyone(payload, axis), axis=0)
    left_rows, basis, q_local = right(all_tokens, outer, payload, raw, error_state)
    block = jnp.sum(exchange(q_local, "outer"), axis=0)
    block = jnp.sum(everyone(block, "replica"), axis=0)
    summed = everyone(block, "outer")
    right_factor, new_error = error(
        all_tokens, workers, payload, basis, summed, raw, error_state
    )
    return (left_rows.transpose(0, 2, 1), right_factor, new_error)


def solution(mesh):
    placed = (
        P(BOTH, None),
        P(BOTH, None),
        P(BOTH),
        P(BOTH, None),
        P(BOTH, None, None, None),
        P(),
    )
    return jax.shard_map(
        local,
        mesh=mesh,
        in_specs=placed,
        out_specs=(P(), P(), P(BOTH, None, None, None)),
        check_vma=False,
    )
```

time: 116 us -> 99.5 us (0.86)
  matrix products: 11.5 us -> 0 us
  other arithmetic: 9.07 us -> 0.11 us
  Pallas kernels: 0 us -> 7.06 us
  local copies, waits for them, and re-layouts: 2.88 us -> 0.85 us
    dot_general x5 -> x0, matrix products: 11.5 us -> none  [the longest x1 4.56 us: local(): jnp.einsum('ghr,grc->ghc', left_factor, right_factor, precision=lax.Preci...]
    pallas_call x0 -> x3, Pallas kernels: none -> 7.06 us  [the longest x1 3.84 us: terms(): pl.pallas_call(terms_kernel, grid=(1,), in_specs=[pl.BlockSpec(memory_spa...]
    reduce_sum x17 -> x1, other arithmetic: 4.43 us -> 0.04 us  [local(): block = jnp.sum(exchange(q_local, 'outer'), axis=0)]
    mul x1 -> x0, other arithmetic: 2.74 us -> none  [local(): merged = factor * raw_full + carried]
where the time goes in v3:
time: 99.5 us; the launch traced here: 99.2 us
  blocking collectives  90.5 us (91%)
  Pallas kernels  7.06 us (7%)
    all_to_all x5, blocking collectives, exchange(): return lax.all_to_all(blocks, axis, 0, 0, tiled=True)  90.5 us
    pallas_call x1, Pallas kernels, terms(): pl.pallas_call(terms_kernel, grid=(1,), in_specs=[pl.BlockSpec(memory_spa...  3.84 us

profile of v3, /device:TPU:1, one launch (start us, length us, event | category | flops | bytes accessed | tf_op | source)
XLA Modules:
  0.0 99.2 jit_solution(4134177963084903883)
XLA Ops:
  0.6 0.0 copy-start
  0.6 3.8 %terms.1 = (bf16[128,4096]{1,0:T(8,128)(2,1)}, f32[16,128]{1,0:T(8,128)}) custom-call(s32[1,8]{1,0:T(1,128)} %len_ref.1, s32[1,128]{1,0:T(1,128)} %bitcast.4, bf16[112,128]{1,0:T(8,128)(2,1)} %bitcast.3, bf16[128,4096]{1,0:T(8,128)(2,1)} %act_ref.1, f32[1,2,56,4096]{3,2,1,0:T(8,128)} %err_ref.5, f32[2,8,4096]{2,1,0:T(8,128)} %warm_ref.1), custom_call_target="tpu_custom_call" | custom-call | tf_op jit(solution)/shard_map/terms/pallas_call | solution.py:166
  4.5 0.0 copy-start.1
  4.5 0.8 broadcast_in_dim.8
  5.3 18.6 %all_to_all.25 = f32[32,16,128]{2,1,0:T(8,128)S(1)} all-to-all(f32[32,16,128]{2,1,0:T(8,128)S(1)} %broadcast_in_dim.8), channel_id=1, replica_groups=mesh['replica'=16,'outer'=32] {'outer'}, dimensions={0} | all-to-all | bytes 524288 | tf_op jit(solution)/shard_map/all_to_all | solution.py:145
  24.0 25.6 %all_to_all.26 = f32[16,16,128]{2,1,0:T(8,128)S(1)} all-to-all(f32[16,16,128]{2,1,0:T(8,128)S(1)} %broadcast_in_dim.9), channel_id=1, replica_groups=mesh['replica'=16,'outer'=32] {'replica'}, dimensions={0} | all-to-all | bytes 262144 | tf_op jit(solution)/shard_map/all_to_all | solution.py:145
  49.6 0.0 copy-done
  49.6 0.0 copy-done.1
  49.6 1.6 %right.1 = (f32[2,8,56]{2,1,0:T(8,128)}, f32[16,128]{1,0:T(8,128)S(1)}, f32[32,16,128]{2,1,0:T(8,128)S(1)}) custom-call(f32[16,128]{1,0:T(8,128)S(1)} %reduce_sum.37.pay_ref, bf16[128,4096]{1,0:T(8,128)(2,1)S(1)} %copy-done.1, f32[1,2,56,4096]{3,2,1,0:T(8,128)S(1)} %copy-done), custom_call_target="tpu_custom_call" | custom-call | tf_op jit(solution)/shard_map/right/pallas_call | solution.py:179
  51.2 15.1 %all_to_all.27 = f32[32,16,128]{2,1,0:T(8,128)S(1)} all-to-all(f32[32,16,128]{2,1,0:T(8,128)S(1)} %get-tuple-element.14), channel_id=1, replica_groups=mesh['replica'=16,'outer'=32] {'outer'}, dimensions={0} | all-to-all | bytes 524288 | tf_op jit(solution)/shard_map/all_to_all | solution.py:145
  66.4 15.9 %all_to_all.28 = f32[16,16,128]{2,1,0:T(8,128)S(1)} all-to-all(f32[16,16,128]{2,1,0:T(8,128)S(1)} %broadcast_in_dim.10), channel_id=1, replica_groups=mesh['replica'=16,'outer'=32] {'replica'}, dimensions={0} | all-to-all | bytes 262144 | tf_op jit(solution)/shard_map/all_to_all | solution.py:145
  82.4 15.1 %all_to_all.29.sum_ref = f32[32,16,128]{2,1,0:T(8,128)S(1)} all-to-all(f32[32,16,128]{2,1,0:T(8,128)S(1)} %broadcast_in_dim.11), channel_id=1, replica_groups=mesh['replica'=16,'outer'=32] {'outer'}, dimensions={0} | all-to-all | bytes 524288 | tf_op jit(solution)/shard_map/all_to_all | solution.py:145
  97.5 1.6 %error.1 = (f32[2,8,4096]{2,1,0:T(8,128)}, f32[1,2,56,4096]{3,2,1,0:T(8,128)}) custom-call(f32[16,128]{1,0:T(8,128)S(1)} %reduce_sum.37.pay_ref, f32[16,128]{1,0:T(8,128)S(1)} %get-tuple-element.13.basis_ref, f32[32,16,128]{2,1,0:T(8,128)S(1)} %all_to_all.29.sum_ref, bf16[128,4096]{1,0:T(8,128)(2,1)S(1)} %copy-done.1, f32[1,2,56,4096]{3,2,1,0:T(8,128)S(1)} %copy-done), custom_call_target="tpu_custom_call" | custom-call | tf_op jit(solution)/shard_map/error/pallas_call | solution.py:197
  (7 shorter events, 0.1 us)
Async XLA Ops:
  0.6 49.0 %copy-start = (f32[1,2,56,4096]{3,2,1,0:T(8,128)S(1)}, f32[1,2,56,4096]{3,2,1,0:T(8,128)}, u32[]{:S(2)}) copy-start(f32[1,2,56,4096]{3,2,1,0:T(8,128)} %err_ref.5) | copy-start | bytes 5505028
  4.5 45.1 %copy-start.1 = (bf16[128,4096]{1,0:T(8,128)(2,1)S(1)}, bf16[128,4096]{1,0:T(8,128)(2,1)}, u32[]{:S(2)}) copy-start(bf16[128,4096]{1,0:T(8,128)(2,1)} %get-tuple-element.11.raw_ref) | copy-start | bytes 3145732

commit v4 on v3

--- a/solution.py
+++ b/solution.py
@@ -5,9 +5,10 @@
 from jax import lax
 from jax.experimental import pallas as pl
 from jax.experimental.pallas import tpu as pltpu
-from jax.sharding import PartitionSpec as P
-
-BOTH = ("replica", "outer")
+from jax.sharding import Mesh, PartitionSpec as P
+
+ALL = ("replica", "chip", "core")
+OUTER = ("chip", "core")
 F32, BF16 = jnp.float32, jnp.bfloat16
 HALF = 64
 TILE = 1024
@@ -59,8 +60,9 @@
     left = lane < HALF
     row = lax.broadcasted_iota(jnp.int32, (rank, 128), 0)
     at_count = jnp.logical_and(row == 0, lane == 127)
-    pay_ref[:rank] = jnp.where(at_count, count, jnp.where(left, of_raw[:rank], of_raw[rank:]))
-    pay_ref[rank:] = jnp.where(left, of_err[:rank], of_err[rank:])
+    top = jnp.where(at_count, count, jnp.where(left, of_raw[:rank], of_raw[rank:]))
+    bottom = jnp.where(left, of_err[:rank], of_err[rank:])
+    pay_ref[...] = jnp.broadcast_to(jnp.concatenate([top, bottom], axis=0)[None], pay_ref.shape)
 
 
 def basis_of(vectors):
@@ -154,11 +156,11 @@
 LIMIT = 16 * 2**20
 
 
-def terms(lengths, labels, grad, activations, error_state, warm_start):
+def terms(copies, lengths, labels, grad, activations, error_state, warm_start):
     _, rank, features = warm_start.shape
     operands = (labels, grad, activations, error_state, warm_start)
     raw = jax.ShapeDtypeStruct((2 * HALF, features), BF16)
-    payload = jax.ShapeDtypeStruct((2 * rank, 128), F32)
+    payload = jax.ShapeDtypeStruct((copies, 2 * rank, 128), F32)
 
     def once(x):
         return pl.BlockSpec(x.shape, lambda i: (0,) * len(x.shape))
@@ -210,18 +212,20 @@
 
 
 def local(activations, grad_hidden, labels, lengths, error_state, warm_start):
-    outer = lax.axis_size("outer")
+    chips = lax.axis_size("chip")
+    outer = 2 * chips
     workers = lax.axis_size("replica") * outer
     all_tokens = float(activations.shape[0] * workers)
     raw, payload = terms(
-        lengths, labels.reshape(1, -1), grad_hidden.T, activations, error_state, warm_start
-    )
-    for axis in ("outer", "replica"):
-        payload = jnp.sum(everyone(payload, axis), axis=0)
+        chips, lengths, labels.reshape(1, -1), grad_hidden.T, activations, error_state, warm_start
+    )
+    half = jnp.sum(exchange(payload.reshape(outer, -1, 128), OUTER), axis=0)
+    half = jnp.sum(everyone(half, "replica"), axis=0)
+    payload = lax.all_gather(half, "core", axis=0, tiled=True)
     left_rows, basis, q_local = right(all_tokens, outer, payload, raw, error_state)
-    block = jnp.sum(exchange(q_local, "outer"), axis=0)
+    block = jnp.sum(exchange(q_local, OUTER), axis=0)
     block = jnp.sum(everyone(block, "replica"), axis=0)
-    summed = everyone(block, "outer")
+    summed = everyone(block, OUTER)
     right_factor, new_error = error(
         all_tokens, workers, payload, basis, summed, raw, error_state
     )
@@ -229,18 +233,20 @@
 
 
 def solution(mesh):
+    replicas, outer = mesh.devices.shape
+    split = Mesh(mesh.devices.reshape(replicas, outer // 2, 2), ("replica", "chip", "core"))
     placed = (
-        P(BOTH, None),
-        P(BOTH, None),
-        P(BOTH),
-        P(BOTH, None),
-        P(BOTH, None, None, None),
+        P(ALL, None),
+        P(ALL, None),
+        P(ALL),
+        P(ALL, None),
+        P(ALL, None, None, None),
         P(),
     )
     return jax.shard_map(
         local,
-        mesh=mesh,
+        mesh=split,
         in_specs=placed,
-        out_specs=(P(), P(), P(BOTH, None, None, None)),
+        out_specs=(P(), P(), P(ALL, None, None, None)),
         check_vma=False,
     )

time: 99.5 us -> 97.8 us (0.983)
  blocking collectives: 90.5 us -> 88.3 us
    all_to_all x5, blocking collectives: 90.5 us -> 84.7 us  [exchange(): return lax.all_to_all(blocks, axis, 0, 0, tiled=True)]
    all_gather x0 -> x1, blocking collectives: none -> 3.59 us  [local(): payload = lax.all_gather(half, 'core', axis=0, tiled=True)]
    unnamed x4 -> x6, local copies, waits for them, and re-layouts: 0.01 us -> 1.23 us
where the time goes in v4:
time: 97.8 us; the launch traced here: 97.5 us
  blocking collectives  88.3 us (90%)
  Pallas kernels  7.13 us (7%)
  local copies, waits for them, and re-layouts  1.27 us (1%)
    all_to_all x5, blocking collectives, exchange(): return lax.all_to_all(blocks, axis, 0, 0, tiled=True)  84.7 us
    pallas_call x1, Pallas kernels, terms(): pl.pallas_call(terms_kernel, grid=(1,), in_specs=[pl.BlockSpec(memory_spa...  3.9 us
    all_gather x1, blocking collectives, local(): payload = lax.all_gather(half, 'core', axis=0, tiled=True)  3.59 us

profile of v4, /device:TPU:1, one launch (start us, length us, event | category | flops | bytes accessed | tf_op | source)
XLA Modules:
  0.0 97.5 jit_solution(5113446117642446858)
XLA Ops:
  0.6 0.0 copy-start
  0.6 3.9 %terms.1 = (bf16[128,4096]{1,0:T(8,128)(2,1)}, f32[16,16,128]{2,1,0:T(8,128)}) custom-call(s32[1,8]{1,0:T(1,128)} %len_ref.1, s32[1,128]{1,0:T(1,128)} %bitcast.6, bf16[112,128]{1,0:T(8,128)(2,1)} %bitcast.5, bf16[128,4096]{1,0:T(8,128)(2,1)} %act_ref.1, f32[1,2,56,4096]{3,2,1,0:T(8,128)} %err_ref.5, f32[2,8,4096]{2,1,0:T(8,128)} %warm_ref.1), custom_call_target="tpu_custom_call" | custom-call | tf_op jit(solution)/shard_map/terms/pallas_call | solution.py:168
  4.5 18.2 %all_to_all.25 = f32[32,8,128]{2,1,0:T(8,128)S(1)} all-to-all(f32[32,8,128]{2,1,0:T(8,128)} %bitcast.4), channel_id=1, replica_groups=mesh['replica'=16,'chip'=16,'core'=2] {'chip','core'}, dimensions={0} | all-to-all | bytes 262144 | tf_op jit(solution)/shard_map/all_to_all | solution.py:147
  22.8 24.4 %all_to_all.26 = f32[16,8,128]{2,1,0:T(8,128)S(1)} all-to-all(f32[16,8,128]{2,1,0:T(8,128)S(1)} %broadcast_in_dim.6), channel_id=1, replica_groups=mesh['replica'=16,'chip'=16,'core'=2] {'replica'}, dimensions={0} | all-to-all | bytes 131072 | tf_op jit(solution)/shard_map/all_to_all | solution.py:147
  47.2 3.6 %all_gather.3.pay_ref = f32[16,128]{1,0:T(8,128)S(1)} all-gather(f32[8,128]{1,0:T(8,128)S(1)} %reduce_sum.37), channel_id=1, replica_groups=mesh['replica'=16,'chip'=16,'core'=2] {'core'}, dimensions={0}, use_global_device_ids=true | all-gather | bytes 12288 | tf_op jit(solution)/shard_map/all_gather | solution.py:224
  50.8 0.0 copy-done
  50.8 0.0 copy-start.1
  50.8 1.2 %copy-done.1 = bf16[128,4096]{1,0:T(8,128)(2,1)S(1)} copy-done((bf16[128,4096]{1,0:T(8,128)(2,1)S(1)}, bf16[128,4096]{1,0:T(8,128)(2,1)}, u32[]{:S(2)}) %copy-start.1) | copy-done | bytes 1048600
  52.0 0.0 copy-start.2
  52.0 1.6 %right.1 = (f32[2,8,56]{2,1,0:T(8,128)}, f32[16,128]{1,0:T(8,128)S(1)}, f32[32,16,128]{2,1,0:T(8,128)S(1)}) custom-call(f32[16,128]{1,0:T(8,128)S(1)} %all_gather.3.pay_ref, bf16[128,4096]{1,0:T(8,128)(2,1)S(1)} %copy-done.1, f32[1,2,56,4096]{3,2,1,0:T(8,128)S(1)} %copy-done), custom_call_target="tpu_custom_call" | custom-call | tf_op jit(solution)/shard_map/right/pallas_call | solution.py:181
  53.6 12.3 %all_to_all.27 = f32[32,16,128]{2,1,0:T(8,128)S(1)} all-to-all(f32[32,16,128]{2,1,0:T(8,128)S(1)} %get-tuple-element.14), channel_id=1, replica_groups=mesh['replica'=16,'chip'=16,'core'=2] {'chip','core'}, dimensions={0} | all-to-all | bytes 524288 | tf_op jit(solution)/shard_map/all_to_all | solution.py:147
  66.0 14.6 %all_to_all.28 = f32[16,16,128]{2,1,0:T(8,128)S(1)} all-to-all(f32[16,16,128]{2,1,0:T(8,128)S(1)} %broadcast_in_dim.7), channel_id=1, replica_groups=mesh['replica'=16,'chip'=16,'core'=2] {'replica'}, dimensions={0} | all-to-all | bytes 262144 | tf_op jit(solution)/shard_map/all_to_all | solution.py:147
  80.7 15.2 %all_to_all.29.sum_ref = f32[32,16,128]{2,1,0:T(8,128)S(1)} all-to-all(f32[32,16,128]{2,1,0:T(8,128)S(1)} %broadcast_in_dim.8), channel_id=1, replica_groups=mesh['replica'=16,'chip'=16,'core'=2] {'chip','core'}, dimensions={0} | all-to-all | bytes 524288 | tf_op jit(solution)/shard_map/all_to_all | solution.py:147
  95.9 0.0 copy-done.2
  95.9 1.6 %error.1 = (f32[2,8,4096]{2,1,0:T(8,128)}, f32[1,2,56,4096]{3,2,1,0:T(8,128)}) custom-call(f32[16,128]{1,0:T(8,128)S(1)} %all_gather.3.pay_ref, f32[16,128]{1,0:T(8,128)S(1)} %get-tuple-element.13.basis_ref, f32[32,16,128]{2,1,0:T(8,128)S(1)} %all_to_all.29.sum_ref, bf16[128,4096]{1,0:T(8,128)(2,1)S(1)} %copy-done.2, f32[1,2,56,4096]{3,2,1,0:T(8,128)S(1)} %copy-done), custom_call_target="tpu_custom_call" | custom-call | tf_op jit(solution)/shard_map/error/pallas_call | solution.py:199
  (7 shorter events, 0.1 us)
Async XLA Ops:
  0.6 50.2 %copy-start = (f32[1,2,56,4096]{3,2,1,0:T(8,128)S(1)}, f32[1,2,56,4096]{3,2,1,0:T(8,128)}, u32[]{:S(2)}) copy-start(f32[1,2,56,4096]{3,2,1,0:T(8,128)} %err_ref.5) | copy-start | bytes 5505028
  50.8 1.2 %copy-start.1 = (bf16[128,4096]{1,0:T(8,128)(2,1)S(1)}, bf16[128,4096]{1,0:T(8,128)(2,1)}, u32[]{:S(2)}) copy-start(bf16[128,4096]{1,0:T(8,128)(2,1)} %get-tuple-element.11.raw_ref) | copy-start | bytes 3145732
  52.0 43.8 %copy-start.2 = (bf16[128,4096]{1,0:T(8,128)(2,1)S(1)}, bf16[128,4096]{1,0:T(8,128)(2,1)}, u32[]{:S(2)}) copy-start(bf16[128,4096]{1,0:T(8,128)(2,1)} %get-tuple-element.11.raw_ref) | copy-start | bytes 3145732

commit v5 on v4

--- a/solution.py
+++ b/solution.py
@@ -32,22 +32,26 @@
     return lax.dot_general(a, b, (((1,), (1,)), ((), ())), preferred_element_type=F32)
 
 
-def terms_kernel(len_ref, label_ref, grad_ref, act_ref, err_ref, warm_ref, raw_ref, pay_ref):
-    hidden = err_ref.shape[2]
+def masked_rows(lengths, labels, grad):
+    documents = lengths.shape[1]
+    square = (documents, documents)
+    upto = lax.broadcasted_iota(jnp.int32, square, 1) <= lax.broadcasted_iota(jnp.int32, square, 0)
+    ends = jnp.sum(jnp.where(upto, lengths.astype(F32), 0.0), axis=1, keepdims=True)
+    place = lax.broadcasted_iota(jnp.int32, (1, labels.shape[1]), 1).astype(F32)
+    at_final = jnp.max(jnp.where(place == ends - 1.0, 1.0, 0.0), axis=0, keepdims=True)
+    mask = jnp.logical_and(labels != -100, at_final == 0.0)
+    hidden = grad.shape[0] // 2
+    grad = grad.astype(F32)
+    rows = padded(grad[:hidden], grad[hidden:])
+    return mask, jnp.where(mask, rows, 0.0).astype(BF16)
+
+
+def terms_kernel(len_ref, label_ref, grad_ref, act_ref, err_ref, warm_ref, pay_ref):
     rank = warm_ref.shape[1]
     n = 2 * rank
-    lane = lax.broadcasted_iota(jnp.int32, (1, 128), 1)
-    mask = label_ref[...] != -100
-    final = -1
-    for document in range(len_ref.shape[1]):
-        final = final + len_ref[0, document]
-        mask = jnp.logical_and(mask, lane != final)
+    mask, masked = masked_rows(len_ref[...], label_ref[...], grad_ref[...])
     count = jnp.sum(mask.astype(F32), axis=1, keepdims=True)
-    grad = grad_ref[...].astype(F32)
-    grad = padded(grad[:hidden], grad[hidden:])
-    masked = jnp.where(mask, grad, 0.0).astype(BF16)
     raw = dot(masked, act_ref[...]).astype(BF16)
-    raw_ref[...] = raw
     warm = warm_ref[...].reshape(n, warm_ref.shape[2])
     high = warm.astype(BF16)
     middle, low = halves(warm - high.astype(F32))
@@ -57,6 +61,7 @@
     carried_high, carried_low = halves(padded(err_ref[0, 0], err_ref[0, 1]))
     of_err = dot_rows(split[: 2 * n], carried_high)
     of_err = of_err[:n] + (of_err[n:] + dot_rows(high, carried_low))
+    lane = lax.broadcasted_iota(jnp.int32, (1, 128), 1)
     left = lane < HALF
     row = lax.broadcasted_iota(jnp.int32, (rank, 128), 0)
     at_count = jnp.logical_and(row == 0, lane == 127)
@@ -81,10 +86,17 @@
     return all_tokens / pay_ref[0:1, 127:128]
 
 
-def right_kernel(all_tokens, pay_ref, raw_ref, err_ref, left_ref, basis_ref, q_ref):
+def right_kernel(
+    all_tokens, pay_ref, len_ref, label_ref, grad_ref, act_ref, err_ref,
+    left_ref, basis_ref, q_ref, raw_ref,
+):
     rank = pay_ref.shape[0] // 2
     hidden = err_ref.shape[2]
     factor = factor_of(pay_ref, all_tokens)
+    _, masked = masked_rows(len_ref[...], label_ref[...], grad_ref[...])
+    for part in range(raw_ref.shape[1] // TILE):
+        at = pl.ds(part * TILE, TILE)
+        raw_ref[:, at] = dot(masked, act_ref[:, at]).astype(BF16)
     lane = lax.broadcasted_iota(jnp.int32, (1, 128), 1)
     p_sum = factor * pay_ref[:rank] + pay_ref[rank:]
     first = basis_of(jnp.where(lane < hidden, p_sum, 0.0))
@@ -110,12 +122,16 @@
 
 
 def error_kernel(
-    all_tokens, workers, pay_ref, basis_ref, sum_ref, raw_ref, err_ref, right_hbm, new_hbm,
-    right_ref, new_ref, sems,
+    all_tokens, workers, pay_ref, basis_ref, sum_ref, len_ref, label_ref, grad_ref, act_ref,
+    err_ref, right_hbm, new_hbm, right_ref, new_ref, raw_ref, sems,
 ):
     rank = pay_ref.shape[0] // 2
     hidden = err_ref.shape[2]
     width = sum_ref.shape[2]
+    _, masked = masked_rows(len_ref[...], label_ref[...], grad_ref[...])
+    for part in range(raw_ref.shape[1] // TILE):
+        at = pl.ds(part * TILE, TILE)
+        raw_ref[:, at] = dot(masked, act_ref[:, at]).astype(BF16)
     high, low = halves(basis_ref[...])
     high, low = high.astype(F32), low.astype(F32)
     gap = jnp.zeros((128 - 6 * rank, 128), F32)
@@ -157,9 +173,8 @@
 
 
 def terms(copies, lengths, labels, grad, activations, error_state, warm_start):
-    _, rank, features = warm_start.shape
-    operands = (labels, grad, activations, error_state, warm_start)
-    raw = jax.ShapeDtypeStruct((2 * HALF, features), BF16)
+    rank = warm_start.shape[1]
+    operands = (lengths, labels, grad, activations, error_state, warm_start)
     payload = jax.ShapeDtypeStruct((copies, 2 * rank, 128), F32)
 
     def once(x):
@@ -168,47 +183,49 @@
     return pl.pallas_call(
         terms_kernel,
         grid=(1,),
-        in_specs=[pl.BlockSpec(memory_space=pltpu.SMEM)] + [once(x) for x in operands],
-        out_specs=[once(raw), once(payload)],
-        out_shape=[raw, payload],
+        in_specs=[once(x) for x in operands],
+        out_specs=once(payload),
+        out_shape=payload,
         name="terms",
-    )(lengths, *operands)
-
-
-def right(all_tokens, outer, payload, raw, error_state):
+    )(*operands)
+
+
+def right(all_tokens, outer, payload, lengths, labels, grad, activations, error_state):
     rank = payload.shape[0] // 2
     hidden, features = error_state.shape[2:]
     return pl.pallas_call(
         functools.partial(right_kernel, all_tokens),
-        in_specs=[VMEM] * 3,
+        in_specs=[VMEM] * 6,
         out_specs=[VMEM] * 3,
         out_shape=[
             jax.ShapeDtypeStruct((2, rank, hidden), F32),
             jax.ShapeDtypeStruct((2 * rank, 128), F32),
             jax.ShapeDtypeStruct((outer, 2 * rank, features // outer), F32),
         ],
+        scratch_shapes=[pltpu.VMEM((2 * HALF, features), BF16)],
         compiler_params=pltpu.CompilerParams(vmem_limit_bytes=LIMIT),
         name="right",
-    )(payload, raw, error_state)
-
-
-def error(all_tokens, workers, payload, basis, summed, raw, error_state):
+    )(payload, lengths, labels, grad, activations, error_state)
+
+
+def error(all_tokens, workers, payload, basis, summed, lengths, labels, grad, activations, error_state):
     rank = payload.shape[0] // 2
     features = error_state.shape[3]
     right_factor = jax.ShapeDtypeStruct((2, rank, features), F32)
     return pl.pallas_call(
         functools.partial(error_kernel, all_tokens, workers),
-        in_specs=[VMEM] * 5,
+        in_specs=[VMEM] * 8,
         out_specs=[ANY] * 2,
         out_shape=[right_factor, jax.ShapeDtypeStruct(error_state.shape, F32)],
         scratch_shapes=[
             pltpu.VMEM(right_factor.shape, F32),
             pltpu.VMEM(error_state.shape, F32),
+            pltpu.VMEM((2 * HALF, features), BF16),
             pltpu.SemaphoreType.DMA((2, features // TILE)),
         ],
         compiler_params=pltpu.CompilerParams(vmem_limit_bytes=LIMIT),
         name="error",
-    )(payload, basis, summed, raw, error_state)
+    )(payload, basis, summed, lengths, labels, grad, activations, error_state)
 
 
 def local(activations, grad_hidden, labels, lengths, error_state, warm_start):
@@ -216,18 +233,17 @@
     outer = 2 * chips
     workers = lax.axis_size("replica") * outer
     all_tokens = float(activations.shape[0] * workers)
-    raw, payload = terms(
-        chips, lengths, labels.reshape(1, -1), grad_hidden.T, activations, error_state, warm_start
-    )
+    tokens = (lengths, labels.reshape(1, -1), grad_hidden.T, activations)
+    payload = terms(chips, *tokens, error_state, warm_start)
     half = jnp.sum(exchange(payload.reshape(outer, -1, 128), OUTER), axis=0)
     half = jnp.sum(everyone(half, "replica"), axis=0)
     payload = lax.all_gather(half, "core", axis=0, tiled=True)
-    left_rows, basis, q_local = right(all_tokens, outer, payload, raw, error_state)
+    left_rows, basis, q_local = right(all_tokens, outer, payload, *tokens, error_state)
     block = jnp.sum(exchange(q_local, OUTER), axis=0)
     block = jnp.sum(everyone(block, "replica"), axis=0)
     summed = everyone(block, OUTER)
     right_factor, new_error = error(
-        all_tokens, workers, payload, basis, summed, raw, error_state
+        all_tokens, workers, payload, basis, summed, *tokens, error_state
     )
     return (left_rows.transpose(0, 2, 1), right_factor, new_error)
 

time: 97.8 us -> 97.1 us (level)
  local copies, waits for them, and re-layouts: 1.27 us -> 0.06 us
    unnamed x6 -> x10, local copies, waits for them, and re-layouts: 1.23 us -> 0.02 us
where the time goes in v5:
time: 97.1 us; the launch traced here: 96.8 us
  blocking collectives  88.3 us (91%)
  Pallas kernels  7.57 us (8%)
    all_to_all x5, blocking collectives, exchange(): return lax.all_to_all(blocks, axis, 0, 0, tiled=True)  84.7 us
    pallas_call x1, Pallas kernels, terms(): pl.pallas_call(terms_kernel, grid=(1,), in_specs=[once(x) for x in operan...  3.97 us
    all_gather x1, blocking collectives, local(): payload = lax.all_gather(half, 'core', axis=0, tiled=True)  3.59 us

profile of v5, /device:TPU:1, one launch (start us, length us, event | category | flops | bytes accessed | tf_op | source)
XLA Modules:
  0.0 96.8 jit_solution(2597547608170066671)
XLA Ops:
  0.6 0.0 copy-start
  0.6 0.0 copy-start.1
  0.7 0.0 copy-start.2
  0.7 0.0 copy-start.3
  0.7 0.0 copy-start.4
  0.7 4.0 %terms.1 = f32[16,16,128]{2,1,0:T(8,128)} custom-call(s32[1,8]{1,0:T(1,128)} %len_ref.5, s32[1,128]{1,0:T(1,128)} %bitcast.7, bf16[112,128]{1,0:T(8,128)(2,1)} %bitcast.4, bf16[128,4096]{1,0:T(8,128)(2,1)} %act_ref.5, f32[1,2,56,4096]{3,2,1,0:T(8,128)} %err_ref.5, f32[2,8,4096]{2,1,0:T(8,128)} %warm_ref.1), custom_call_target="tpu_custom_call" | custom-call | tf_op jit(solution)/shard_map/terms/pallas_call | solution.py:183
  4.7 18.2 %all_to_all.25 = f32[32,8,128]{2,1,0:T(8,128)S(1)} all-to-all(f32[32,8,128]{2,1,0:T(8,128)} %bitcast.10), channel_id=1, replica_groups=mesh['replica'=16,'chip'=16,'core'=2] {'chip','core'}, dimensions={0} | all-to-all | bytes 262144 | tf_op jit(solution)/shard_map/all_to_all | solution.py:163
  22.9 24.4 %all_to_all.26 = f32[16,8,128]{2,1,0:T(8,128)S(1)} all-to-all(f32[16,8,128]{2,1,0:T(8,128)S(1)} %broadcast_in_dim.6), channel_id=1, replica_groups=mesh['replica'=16,'chip'=16,'core'=2] {'replica'}, dimensions={0} | all-to-all | bytes 131072 | tf_op jit(solution)/shard_map/all_to_all | solution.py:163
  47.3 3.6 %all_gather.3.pay_ref = f32[16,128]{1,0:T(8,128)S(1)} all-gather(f32[8,128]{1,0:T(8,128)S(1)} %reduce_sum.37), channel_id=1, replica_groups=mesh['replica'=16,'chip'=16,'core'=2] {'core'}, dimensions={0}, use_global_device_ids=true | all-gather | bytes 12288 | tf_op jit(solution)/shard_map/all_gather | solution.py:240
  50.9 0.0 copy-done
  50.9 0.0 copy-done.1
  50.9 0.0 copy-done.2
  50.9 0.0 copy-done.3
  50.9 0.0 copy-done.4
  50.9 1.7 %right.1 = (f32[2,8,56]{2,1,0:T(8,128)}, f32[16,128]{1,0:T(8,128)S(1)}, f32[32,16,128]{2,1,0:T(8,128)S(1)}) custom-call(f32[16,128]{1,0:T(8,128)S(1)} %all_gather.3.pay_ref, s32[1,8]{1,0:T(1,128)S(1)} %copy-done.3, s32[1,128]{1,0:T(1,128)S(1)} %bitcast.8, bf16[112,128]{1,0:T(8,128)(2,1)S(1)} %bitcast.5, bf16[128,4096]{1,0:T(8,128)(2,1)S(1)} %copy-done.1, ...), custom_call_target="tpu_custom_call" | custom-call | tf_op jit(solution)/shard_map/right/pallas_call | solution.py:196
  52.6 12.3 %all_to_all.27 = f32[32,16,128]{2,1,0:T(8,128)S(1)} all-to-all(f32[32,16,128]{2,1,0:T(8,128)S(1)} %get-tuple-element.10), channel_id=1, replica_groups=mesh['replica'=16,'chip'=16,'core'=2] {'chip','core'}, dimensions={0} | all-to-all | bytes 524288 | tf_op jit(solution)/shard_map/all_to_all | solution.py:163
  65.0 14.6 %all_to_all.28 = f32[16,16,128]{2,1,0:T(8,128)S(1)} all-to-all(f32[16,16,128]{2,1,0:T(8,128)S(1)} %broadcast_in_dim.7), channel_id=1, replica_groups=mesh['replica'=16,'chip'=16,'core'=2] {'replica'}, dimensions={0} | all-to-all | bytes 262144 | tf_op jit(solution)/shard_map/all_to_all | solution.py:163
  79.7 15.2 %all_to_all.29.sum_ref = f32[32,16,128]{2,1,0:T(8,128)S(1)} all-to-all(f32[32,16,128]{2,1,0:T(8,128)S(1)} %broadcast_in_dim.8), channel_id=1, replica_groups=mesh['replica'=16,'chip'=16,'core'=2] {'chip','core'}, dimensions={0} | all-to-all | bytes 524288 | tf_op jit(solution)/shard_map/all_to_all | solution.py:163
  94.9 1.9 %error.1 = (f32[2,8,4096]{2,1,0:T(8,128)}, f32[1,2,56,4096]{3,2,1,0:T(8,128)}) custom-call(f32[16,128]{1,0:T(8,128)S(1)} %all_gather.3.pay_ref, f32[16,128]{1,0:T(8,128)S(1)} %get-tuple-element.9.basis_ref, f32[32,16,128]{2,1,0:T(8,128)S(1)} %all_to_all.29.sum_ref, s32[1,8]{1,0:T(1,128)S(1)} %copy-done.3, s32[1,128]{1,0:T(1,128)S(1)} %bitcast.9, ...), custom_call_target="tpu_custom_call" | custom-call | tf_op jit(solution)/shard_map/error/pallas_call | solution.py:215
  (7 shorter events, 0.1 us)
Async XLA Ops:
  0.6 50.3 %copy-start = (f32[1,2,56,4096]{3,2,1,0:T(8,128)S(1)}, f32[1,2,56,4096]{3,2,1,0:T(8,128)}, u32[]{:S(2)}) copy-start(f32[1,2,56,4096]{3,2,1,0:T(8,128)} %err_ref.5) | copy-start | bytes 5505028
  0.6 50.3 %copy-start.1 = (bf16[128,4096]{1,0:T(8,128)(2,1)S(1)}, bf16[128,4096]{1,0:T(8,128)(2,1)}, u32[]{:S(2)}) copy-start(bf16[128,4096]{1,0:T(8,128)(2,1)} %act_ref.5) | copy-start | bytes 3145732
  0.7 50.3 %copy-start.2 = (bf16[128,112]{0,1:T(8,128)(2,1)S(1)}, bf16[128,112]{0,1:T(8,128)(2,1)}, u32[]{:S(2)}) copy-start(bf16[128,112]{0,1:T(8,128)(2,1)} %param.7) | copy-start | bytes 86020
  0.7 50.3 %copy-start.3 = (s32[1,8]{1,0:T(1,128)S(1)}, s32[1,8]{1,0:T(1,128)}, u32[]{:S(2)}) copy-start(s32[1,8]{1,0:T(1,128)} %len_ref.5) | copy-start | bytes 100
  0.7 50.3 %copy-start.4 = (s32[128]{0:T(128)S(1)}, s32[128]{0:T(128)}, u32[]{:S(2)}) copy-start(s32[128]{0:T(128)} %param.8) | copy-start | bytes 1540

commit v6 on v5

--- a/solution.py
+++ b/solution.py
@@ -88,7 +88,7 @@
 
 def right_kernel(
     all_tokens, pay_ref, len_ref, label_ref, grad_ref, act_ref, err_ref,
-    left_ref, basis_ref, q_ref, raw_ref,
+    basis_ref, q_ref, raw_ref,
 ):
     rank = pay_ref.shape[0] // 2
     hidden = err_ref.shape[2]
@@ -102,8 +102,6 @@
     first = basis_of(jnp.where(lane < hidden, p_sum, 0.0))
     of_second = jnp.logical_and(lane >= HALF, lane < HALF + hidden)
     second = basis_of(jnp.where(of_second, p_sum, 0.0))
-    left_ref[0] = first[:, :hidden]
-    left_ref[1] = pltpu.roll(second, HALF, 1)[:, :hidden]
     basis = jnp.concatenate([first, second], axis=0)
     basis_ref[...] = basis
     high, low = halves(basis)
@@ -123,23 +121,25 @@
 
 def error_kernel(
     all_tokens, workers, pay_ref, basis_ref, sum_ref, len_ref, label_ref, grad_ref, act_ref,
-    err_ref, right_hbm, new_hbm, right_ref, new_ref, raw_ref, sems,
+    err_ref, left_hbm, right_hbm, new_hbm, left_ref, right_ref, new_ref, sems,
 ):
     rank = pay_ref.shape[0] // 2
     hidden = err_ref.shape[2]
     width = sum_ref.shape[2]
     _, masked = masked_rows(len_ref[...], label_ref[...], grad_ref[...])
-    for part in range(raw_ref.shape[1] // TILE):
-        at = pl.ds(part * TILE, TILE)
-        raw_ref[:, at] = dot(masked, act_ref[:, at]).astype(BF16)
-    high, low = halves(basis_ref[...])
+    basis = basis_ref[...]
+    left_ref[0] = basis[:rank, :hidden]
+    left_ref[1] = pltpu.roll(basis[rank:], HALF, 1)[:, :hidden]
+    copies = [pltpu.make_async_copy(left_ref, left_hbm, sems.at[2, 0])]
+    copies[0].start()
+    high, low = halves(basis)
     high, low = high.astype(F32), low.astype(F32)
     gap = jnp.zeros((128 - 6 * rank, 128), F32)
     lhs = jnp.concatenate([high, high, low, gap], axis=0).T.astype(BF16)
     factor = factor_of(pay_ref, all_tokens)
-    copies = []
-    for part in range(raw_ref.shape[1] // TILE):
+    for part in range(act_ref.shape[1] // TILE):
         at = pl.ds(part * TILE, TILE)
+        full = dot(masked, act_ref[:, at]).astype(BF16).astype(F32)
         blocks = TILE // width
         summed = jnp.concatenate([sum_ref[part * blocks + block] for block in range(blocks)], axis=1)
         right_ref[0, :, at] = summed[:rank]
@@ -151,7 +151,7 @@
         approx = dot(lhs, jnp.concatenate([high, low, high, gap], axis=0))
         for matrix in range(2):
             rows = slice(matrix * HALF, matrix * HALF + HALF)
-            raw = raw_ref[rows, at].astype(F32)[:hidden]
+            raw = full[rows][:hidden]
             new_ref[0, matrix, :, at] = factor * raw + err_ref[0, matrix, :, at] - approx[rows][:hidden]
         copies.append(pltpu.make_async_copy(new_ref.at[:, :, :, at], new_hbm.at[:, :, :, at], sems.at[1, part]))
         copies[-1].start()
@@ -192,13 +192,12 @@
 
 def right(all_tokens, outer, payload, lengths, labels, grad, activations, error_state):
     rank = payload.shape[0] // 2
-    hidden, features = error_state.shape[2:]
+    features = error_state.shape[3]
     return pl.pallas_call(
         functools.partial(right_kernel, all_tokens),
         in_specs=[VMEM] * 6,
-        out_specs=[VMEM] * 3,
+        out_specs=[VMEM] * 2,
         out_shape=[
-            jax.ShapeDtypeStruct((2, rank, hidden), F32),
             jax.ShapeDtypeStruct((2 * rank, 128), F32),
             jax.ShapeDtypeStruct((outer, 2 * rank, features // outer), F32),
         ],
@@ -210,18 +209,19 @@
 
 def error(all_tokens, workers, payload, basis, summed, lengths, labels, grad, activations, error_state):
     rank = payload.shape[0] // 2
-    features = error_state.shape[3]
+    hidden, features = error_state.shape[2:]
+    left_factor = jax.ShapeDtypeStruct((2, rank, hidden), F32)
     right_factor = jax.ShapeDtypeStruct((2, rank, features), F32)
     return pl.pallas_call(
         functools.partial(error_kernel, all_tokens, workers),
         in_specs=[VMEM] * 8,
-        out_specs=[ANY] * 2,
-        out_shape=[right_factor, jax.ShapeDtypeStruct(error_state.shape, F32)],
+        out_specs=[ANY] * 3,
+        out_shape=[left_factor, right_factor, jax.ShapeDtypeStruct(error_state.shape, F32)],
         scratch_shapes=[
+            pltpu.VMEM(left_factor.shape, F32),
             pltpu.VMEM(right_factor.shape, F32),
             pltpu.VMEM(error_state.shape, F32),
-            pltpu.VMEM((2 * HALF, features), BF16),
-            pltpu.SemaphoreType.DMA((2, features // TILE)),
+            pltpu.SemaphoreType.DMA((3, features // TILE)),
         ],
         compiler_params=pltpu.CompilerParams(vmem_limit_bytes=LIMIT),
         name="error",
@@ -238,11 +238,11 @@
     half = jnp.sum(exchange(payload.reshape(outer, -1, 128), OUTER), axis=0)
     half = jnp.sum(everyone(half, "replica"), axis=0)
     payload = lax.all_gather(half, "core", axis=0, tiled=True)
-    left_rows, basis, q_local = right(all_tokens, outer, payload, *tokens, error_state)
+    basis, q_local = right(all_tokens, outer, payload, *tokens, error_state)
     block = jnp.sum(exchange(q_local, OUTER), axis=0)
     block = jnp.sum(everyone(block, "replica"), axis=0)
     summed = everyone(block, OUTER)
-    right_factor, new_error = error(
+    left_rows, right_factor, new_error = error(
         all_tokens, workers, payload, basis, summed, *tokens, error_state
     )
     return (left_rows.transpose(0, 2, 1), right_factor, new_error)

time: 97.1 us -> 96.7 us (level)
  no operation moved by 1% of the time
where the time goes in v6:
time: 96.7 us; the launch traced here: 96.4 us
  blocking collectives  88.3 us (91%)
  Pallas kernels  7.16 us (7%)
    all_to_all x5, blocking collectives, exchange(): return lax.all_to_all(blocks, axis, 0, 0, tiled=True)  84.7 us
    pallas_call x1, Pallas kernels, terms(): pl.pallas_call(terms_kernel, grid=(1,), in_specs=[once(x) for x in operan...  3.97 us
    all_gather x1, blocking collectives, local(): payload = lax.all_gather(half, 'core', axis=0, tiled=True)  3.59 us

profile of v6, /device:TPU:1, one launch (start us, length us, event | category | flops | bytes accessed | tf_op | source)
XLA Modules:
  0.0 96.4 jit_solution(12332789924307294006)
XLA Ops:
  0.6 0.0 copy-start
  0.6 0.0 copy-start.1
  0.7 0.0 copy-start.2
  0.7 0.0 copy-start.3
  0.7 0.0 copy-start.4
  0.7 4.0 %terms.1 = f32[16,16,128]{2,1,0:T(8,128)} custom-call(s32[1,8]{1,0:T(1,128)} %len_ref.5, s32[1,128]{1,0:T(1,128)} %bitcast.7, bf16[112,128]{1,0:T(8,128)(2,1)} %bitcast.4, bf16[128,4096]{1,0:T(8,128)(2,1)} %act_ref.5, f32[1,2,56,4096]{3,2,1,0:T(8,128)} %err_ref.5, f32[2,8,4096]{2,1,0:T(8,128)} %warm_ref.1), custom_call_target="tpu_custom_call" | custom-call | tf_op jit(solution)/shard_map/terms/pallas_call | solution.py:183
  4.7 18.2 %all_to_all.25 = f32[32,8,128]{2,1,0:T(8,128)S(1)} all-to-all(f32[32,8,128]{2,1,0:T(8,128)} %bitcast.10), channel_id=1, replica_groups=mesh['replica'=16,'chip'=16,'core'=2] {'chip','core'}, dimensions={0} | all-to-all | bytes 262144 | tf_op jit(solution)/shard_map/all_to_all | solution.py:163
  22.9 24.4 %all_to_all.26 = f32[16,8,128]{2,1,0:T(8,128)S(1)} all-to-all(f32[16,8,128]{2,1,0:T(8,128)S(1)} %broadcast_in_dim.6), channel_id=1, replica_groups=mesh['replica'=16,'chip'=16,'core'=2] {'replica'}, dimensions={0} | all-to-all | bytes 131072 | tf_op jit(solution)/shard_map/all_to_all | solution.py:163
  47.3 3.6 %all_gather.3.pay_ref = f32[16,128]{1,0:T(8,128)S(1)} all-gather(f32[8,128]{1,0:T(8,128)S(1)} %reduce_sum.37), channel_id=1, replica_groups=mesh['replica'=16,'chip'=16,'core'=2] {'core'}, dimensions={0}, use_global_device_ids=true | all-gather | bytes 12288 | tf_op jit(solution)/shard_map/all_gather | solution.py:240
  50.9 0.0 copy-done
  50.9 0.0 copy-done.1
  50.9 0.0 copy-done.2
  50.9 0.0 copy-done.3
  50.9 0.0 copy-done.4
  50.9 1.4 %right.1 = (f32[16,128]{1,0:T(8,128)S(1)}, f32[32,16,128]{2,1,0:T(8,128)S(1)}) custom-call(f32[16,128]{1,0:T(8,128)S(1)} %all_gather.3.pay_ref, s32[1,8]{1,0:T(1,128)S(1)} %copy-done.3, s32[1,128]{1,0:T(1,128)S(1)} %bitcast.8, bf16[112,128]{1,0:T(8,128)(2,1)S(1)} %bitcast.5, bf16[128,4096]{1,0:T(8,128)(2,1)S(1)} %copy-done.1, f32[1,2,56,4096]{3,2,1,0:T(8,128)S(1)} %copy-done), custom_call_target="tpu_custom_call" | custom-call | tf_op jit(solution)/shard_map/right/pallas_call | solution.py:196
  52.3 12.3 %all_to_all.27 = f32[32,16,128]{2,1,0:T(8,128)S(1)} all-to-all(f32[32,16,128]{2,1,0:T(8,128)S(1)} %get-tuple-element.9), channel_id=1, replica_groups=mesh['replica'=16,'chip'=16,'core'=2] {'chip','core'}, dimensions={0} | all-to-all | bytes 524288 | tf_op jit(solution)/shard_map/all_to_all | solution.py:163
  64.7 14.6 %all_to_all.28 = f32[16,16,128]{2,1,0:T(8,128)S(1)} all-to-all(f32[16,16,128]{2,1,0:T(8,128)S(1)} %broadcast_in_dim.7), channel_id=1, replica_groups=mesh['replica'=16,'chip'=16,'core'=2] {'replica'}, dimensions={0} | all-to-all | bytes 262144 | tf_op jit(solution)/shard_map/all_to_all | solution.py:163
  79.4 15.2 %all_to_all.29.sum_ref = f32[32,16,128]{2,1,0:T(8,128)S(1)} all-to-all(f32[32,16,128]{2,1,0:T(8,128)S(1)} %broadcast_in_dim.8), channel_id=1, replica_groups=mesh['replica'=16,'chip'=16,'core'=2] {'chip','core'}, dimensions={0} | all-to-all | bytes 524288 | tf_op jit(solution)/shard_map/all_to_all | solution.py:163
  94.6 1.8 %error.1 = (f32[2,8,56]{2,1,0:T(8,128)}, f32[2,8,4096]{2,1,0:T(8,128)}, f32[1,2,56,4096]{3,2,1,0:T(8,128)}) custom-call(f32[16,128]{1,0:T(8,128)S(1)} %all_gather.3.pay_ref, f32[16,128]{1,0:T(8,128)S(1)} %get-tuple-element.8.basis_ref, f32[32,16,128]{2,1,0:T(8,128)S(1)} %all_to_all.29.sum_ref, s32[1,8]{1,0:T(1,128)S(1)} %copy-done.3, s32[1,128]{1,0:T(1,128)S(1)} %bitcast.9, ...), custom_call_target="tpu_custom_call" | custom-call | tf_op jit(solution)/shard_map/error/pallas_call | solution.py:215
  (7 shorter events, 0.1 us)
Async XLA Ops:
  0.6 50.3 %copy-start = (f32[1,2,56,4096]{3,2,1,0:T(8,128)S(1)}, f32[1,2,56,4096]{3,2,1,0:T(8,128)}, u32[]{:S(2)}) copy-start(f32[1,2,56,4096]{3,2,1,0:T(8,128)} %err_ref.5) | copy-start | bytes 5505028
  0.6 50.3 %copy-start.1 = (bf16[128,4096]{1,0:T(8,128)(2,1)S(1)}, bf16[128,4096]{1,0:T(8,128)(2,1)}, u32[]{:S(2)}) copy-start(bf16[128,4096]{1,0:T(8,128)(2,1)} %act_ref.5) | copy-start | bytes 3145732
  0.7 50.3 %copy-start.2 = (bf16[128,112]{0,1:T(8,128)(2,1)S(1)}, bf16[128,112]{0,1:T(8,128)(2,1)}, u32[]{:S(2)}) copy-start(bf16[128,112]{0,1:T(8,128)(2,1)} %param.7) | copy-start | bytes 86020
  0.7 50.3 %copy-start.3 = (s32[1,8]{1,0:T(1,128)S(1)}, s32[1,8]{1,0:T(1,128)}, u32[]{:S(2)}) copy-start(s32[1,8]{1,0:T(1,128)} %len_ref.5) | copy-start | bytes 100
  0.7 50.3 %copy-start.4 = (s32[128]{0:T(128)S(1)}, s32[128]{0:T(128)}, u32[]{:S(2)}) copy-start(s32[128]{0:T(128)} %param.8) | copy-start | bytes 1540

commit v7 on v6

--- a/solution.py
+++ b/solution.py
@@ -7,8 +7,10 @@
 from jax.experimental.pallas import tpu as pltpu
 from jax.sharding import Mesh, PartitionSpec as P
 
-ALL = ("replica", "chip", "core")
+ALL = ("far", "near", "chip", "core")
+REPLICA = ("far", "near")
 OUTER = ("chip", "core")
+PAIR = ("near", "chip", "core")
 F32, BF16 = jnp.float32, jnp.bfloat16
 HALF = 64
 TILE = 1024
@@ -108,7 +110,7 @@
     top = jnp.concatenate([high, high], axis=1)
     bottom = jnp.concatenate([low, jnp.zeros_like(low)], axis=1)
     lhs = jnp.concatenate([top, bottom], axis=0)
-    width = q_ref.shape[2]
+    width = q_ref.shape[3]
     for part in range(raw_ref.shape[1] // TILE):
         at = pl.ds(part * TILE, TILE)
         carried = padded(err_ref[0, 0, :, at], err_ref[0, 1, :, at])
@@ -116,7 +118,9 @@
         both = dot(lhs, jnp.concatenate([high, low], axis=0))
         q_local = both[: 2 * rank] + both[2 * rank :]
         for block in range(TILE // width):
-            q_ref[part * (TILE // width) + block] = q_local[:, block * width : (block + 1) * width]
+            columns = q_local[:, block * width : (block + 1) * width]
+            q_ref[0, part * (TILE // width) + block] = columns[:rank]
+            q_ref[1, part * (TILE // width) + block] = columns[rank:]
 
 
 def error_kernel(
@@ -125,7 +129,7 @@
 ):
     rank = pay_ref.shape[0] // 2
     hidden = err_ref.shape[2]
-    width = sum_ref.shape[2]
+    width = sum_ref.shape[3]
     _, masked = masked_rows(len_ref[...], label_ref[...], grad_ref[...])
     basis = basis_ref[...]
     left_ref[0] = basis[:rank, :hidden]
@@ -141,7 +145,11 @@
         at = pl.ds(part * TILE, TILE)
         full = dot(masked, act_ref[:, at]).astype(BF16).astype(F32)
         blocks = TILE // width
-        summed = jnp.concatenate([sum_ref[part * blocks + block] for block in range(blocks)], axis=1)
+        summed = [
+            jnp.concatenate([sum_ref[matrix, part * blocks + block] for block in range(blocks)], axis=1)
+            for matrix in range(2)
+        ]
+        summed = jnp.concatenate(summed, axis=0)
         right_ref[0, :, at] = summed[:rank]
         right_ref[1, :, at] = summed[rank:]
         copies.append(pltpu.make_async_copy(right_ref.at[:, :, at], right_hbm.at[:, :, at], sems.at[0, part]))
@@ -199,7 +207,7 @@
         out_specs=[VMEM] * 2,
         out_shape=[
             jax.ShapeDtypeStruct((2 * rank, 128), F32),
-            jax.ShapeDtypeStruct((outer, 2 * rank, features // outer), F32),
+            jax.ShapeDtypeStruct((2, outer, rank, features // outer), F32),
         ],
         scratch_shapes=[pltpu.VMEM((2 * HALF, features), BF16)],
         compiler_params=pltpu.CompilerParams(vmem_limit_bytes=LIMIT),
@@ -231,17 +239,18 @@
 def local(activations, grad_hidden, labels, lengths, error_state, warm_start):
     chips = lax.axis_size("chip")
     outer = 2 * chips
-    workers = lax.axis_size("replica") * outer
+    workers = lax.axis_size(ALL)
     all_tokens = float(activations.shape[0] * workers)
     tokens = (lengths, labels.reshape(1, -1), grad_hidden.T, activations)
     payload = terms(chips, *tokens, error_state, warm_start)
     half = jnp.sum(exchange(payload.reshape(outer, -1, 128), OUTER), axis=0)
-    half = jnp.sum(everyone(half, "replica"), axis=0)
+    half = jnp.sum(everyone(half, REPLICA), axis=0)
     payload = lax.all_gather(half, "core", axis=0, tiled=True)
     basis, q_local = right(all_tokens, outer, payload, *tokens, error_state)
-    block = jnp.sum(exchange(q_local, OUTER), axis=0)
-    block = jnp.sum(everyone(block, "replica"), axis=0)
-    summed = everyone(block, OUTER)
+    _, _, rank, width = q_local.shape
+    block = jnp.sum(exchange(q_local.reshape(-1, rank, width), PAIR), axis=0)
+    block = jnp.sum(everyone(block, "far"), axis=0)
+    summed = everyone(block, PAIR).reshape(q_local.shape)
     left_rows, right_factor, new_error = error(
         all_tokens, workers, payload, basis, summed, *tokens, error_state
     )
@@ -250,7 +259,7 @@
 
 def solution(mesh):
     replicas, outer = mesh.devices.shape
-    split = Mesh(mesh.devices.reshape(replicas, outer // 2, 2), ("replica", "chip", "core"))
+    split = Mesh(mesh.devices.reshape(replicas // 2, 2, outer // 2, 2), ALL)
     placed = (
         P(ALL, None),
         P(ALL, None),

time: 96.7 us -> 98.3 us (1.017)
  blocking collectives: 88.3 us -> 89.9 us
    all_to_all x5, blocking collectives: 84.7 us -> 86.3 us  [exchange(): return lax.all_to_all(blocks, axis, 0, 0, tiled=True)]
where the time goes in v7:
time: 98.3 us; the launch traced here: 98 us
  blocking collectives  89.9 us (91%)
  Pallas kernels  7.16 us (7%)
    all_to_all x5, blocking collectives, exchange(): return lax.all_to_all(blocks, axis, 0, 0, tiled=True)  86.3 us
    pallas_call x1, Pallas kernels, terms(): pl.pallas_call(terms_kernel, grid=(1,), in_specs=[once(x) for x in operan...  3.97 us
    all_gather x1, blocking collectives, local(): payload = lax.all_gather(half, 'core', axis=0, tiled=True)  3.59 us

profile of v7, /device:TPU:1, one launch (start us, length us, event | category | flops | bytes accessed | tf_op | source)
XLA Modules:
  0.0 98.0 jit_solution(15841701970518099748)
XLA Ops:
  0.6 0.0 copy-start
  0.6 0.0 copy-start.1
  0.7 0.0 copy-start.2
  0.7 0.0 copy-start.3
  0.7 0.0 copy-start.4
  0.7 4.0 %terms.1 = f32[16,16,128]{2,1,0:T(8,128)} custom-call(s32[1,8]{1,0:T(1,128)} %len_ref.5, s32[1,128]{1,0:T(1,128)} %bitcast.11, bf16[112,128]{1,0:T(8,128)(2,1)} %bitcast.8, bf16[128,4096]{1,0:T(8,128)(2,1)} %act_ref.5, f32[1,2,56,4096]{3,2,1,0:T(8,128)} %err_ref.5, f32[2,8,4096]{2,1,0:T(8,128)} %warm_ref.1), custom_call_target="tpu_custom_call" | custom-call | tf_op jit(solution)/shard_map/terms/pallas_call | solution.py:191
  4.7 18.2 %all_to_all.25 = f32[32,8,128]{2,1,0:T(8,128)S(1)} all-to-all(f32[32,8,128]{2,1,0:T(8,128)} %bitcast.14), channel_id=1, replica_groups=mesh['far'=8,'near'=2,'chip'=16,'core'=2] {'chip','core'}, dimensions={0} | all-to-all | bytes 262144 | tf_op jit(solution)/shard_map/all_to_all | solution.py:171
  22.9 24.4 %all_to_all.26 = f32[16,8,128]{2,1,0:T(8,128)S(1)} all-to-all(f32[16,8,128]{2,1,0:T(8,128)S(1)} %broadcast_in_dim.6), channel_id=1, replica_groups=mesh['far'=8,'near'=2,'chip'=16,'core'=2] {'far','near'}, dimensions={0} | all-to-all | bytes 131072 | tf_op jit(solution)/shard_map/all_to_all | solution.py:171
  47.3 3.6 %all_gather.3.pay_ref = f32[16,128]{1,0:T(8,128)S(1)} all-gather(f32[8,128]{1,0:T(8,128)S(1)} %reduce_sum.37), channel_id=1, replica_groups=mesh['far'=8,'near'=2,'chip'=16,'core'=2] {'core'}, dimensions={0}, use_global_device_ids=true | all-gather | bytes 12288 | tf_op jit(solution)/shard_map/all_gather | solution.py:248
  50.9 0.0 copy-done
  50.9 0.0 copy-done.1
  50.9 0.0 copy-done.2
  50.9 0.0 copy-done.3
  50.9 0.0 copy-done.4
  50.9 1.4 %right.1 = (f32[16,128]{1,0:T(8,128)S(1)}, f32[2,32,8,128]{3,2,1,0:T(8,128)S(1)}) custom-call(f32[16,128]{1,0:T(8,128)S(1)} %all_gather.3.pay_ref, s32[1,8]{1,0:T(1,128)S(1)} %copy-done.3, s32[1,128]{1,0:T(1,128)S(1)} %bitcast.12, bf16[112,128]{1,0:T(8,128)(2,1)S(1)} %bitcast.9, bf16[128,4096]{1,0:T(8,128)(2,1)S(1)} %copy-done.1, f32[1,2,56,4096]{3,2,1,0:T(8,128)S(1)} %copy-done), custom_call_target="tpu_custom_call" | custom-call | tf_op jit(solution)/shard_map/right/pallas_call | solution.py:204
  52.3 13.9 %all_to_all.27 = f32[64,8,128]{2,1,0:T(8,128)S(1)} all-to-all(f32[64,8,128]{2,1,0:T(8,128)S(1)} %bitcast.7), channel_id=1, replica_groups=mesh['far'=8,'near'=2,'chip'=16,'core'=2] {'near','chip','core'}, dimensions={0} | all-to-all | bytes 524288 | tf_op jit(solution)/shard_map/all_to_all | solution.py:171
  66.3 0.1 reduce_sum.38
  66.3 14.5 %all_to_all.28 = f32[8,8,128]{2,1,0:T(8,128)S(1)} all-to-all(f32[8,8,128]{2,1,0:T(8,128)S(1)} %broadcast_in_dim.7), channel_id=1, replica_groups=mesh['far'=8,'near'=2,'chip'=16,'core'=2] {'far'}, dimensions={0} | all-to-all | bytes 65536 | tf_op jit(solution)/shard_map/all_to_all | solution.py:171
  80.9 15.3 %all_to_all.29 = f32[64,8,128]{2,1,0:T(8,128)S(1)} all-to-all(f32[64,8,128]{2,1,0:T(8,128)S(1)} %broadcast_in_dim.8), channel_id=1, replica_groups=mesh['far'=8,'near'=2,'chip'=16,'core'=2] {'near','chip','core'}, dimensions={0} | all-to-all | bytes 524288 | tf_op jit(solution)/shard_map/all_to_all | solution.py:171
  96.2 1.8 %error.1 = (f32[2,8,56]{2,1,0:T(8,128)}, f32[2,8,4096]{2,1,0:T(8,128)}, f32[1,2,56,4096]{3,2,1,0:T(8,128)}) custom-call(f32[16,128]{1,0:T(8,128)S(1)} %all_gather.3.pay_ref, f32[16,128]{1,0:T(8,128)S(1)} %get-tuple-element.8.basis_ref, f32[2,32,8,128]{3,2,1,0:T(8,128)S(1)} %bitcast.6, s32[1,8]{1,0:T(1,128)S(1)} %copy-done.3, s32[1,128]{1,0:T(1,128)S(1)} %bitcast.13, ...), custom_call_target="tpu_custom_call" | custom-call | tf_op jit(solution)/shard_map/error/pallas_call | solution.py:223
  (6 shorter events, 0.1 us)
Async XLA Ops:
  0.6 50.3 %copy-start = (f32[1,2,56,4096]{3,2,1,0:T(8,128)S(1)}, f32[1,2,56,4096]{3,2,1,0:T(8,128)}, u32[]{:S(2)}) copy-start(f32[1,2,56,4096]{3,2,1,0:T(8,128)} %err_ref.5) | copy-start | bytes 5505028
  0.6 50.3 %copy-start.1 = (bf16[128,4096]{1,0:T(8,128)(2,1)S(1)}, bf16[128,4096]{1,0:T(8,128)(2,1)}, u32[]{:S(2)}) copy-start(bf16[128,4096]{1,0:T(8,128)(2,1)} %act_ref.5) | copy-start | bytes 3145732
  0.7 50.3 %copy-start.2 = (bf16[128,112]{0,1:T(8,128)(2,1)S(1)}, bf16[128,112]{0,1:T(8,128)(2,1)}, u32[]{:S(2)}) copy-start(bf16[128,112]{0,1:T(8,128)(2,1)} %param.7) | copy-start | bytes 86020
  0.7 50.3 %copy-start.3 = (s32[1,8]{1,0:T(1,128)S(1)}, s32[1,8]{1,0:T(1,128)}, u32[]{:S(2)}) copy-start(s32[1,8]{1,0:T(1,128)} %len_ref.5) | copy-start | bytes 100
  0.7 50.3 %copy-start.4 = (s32[128]{0:T(128)S(1)}, s32[128]{0:T(128)}, u32[]{:S(2)}) copy-start(s32[128]{0:T(128)} %param.8) | copy-start | bytes 1540

commit v8 on v6

--- a/solution.py
+++ b/solution.py
@@ -54,12 +54,11 @@
     raw = dot(masked, act_ref[...]).astype(BF16)
     warm = warm_ref[...].reshape(n, warm_ref.shape[2])
     high = warm.astype(BF16)
-    middle, low = halves(warm - high.astype(F32))
-    split = jnp.concatenate([high, middle, low], axis=0)
+    split = jnp.concatenate([high, (warm - high.astype(F32)).astype(BF16)], axis=0)
     of_raw = dot_rows(split, raw)
-    of_raw = of_raw[:n] + (of_raw[n : 2 * n] + of_raw[2 * n :])
+    of_raw = of_raw[:n] + of_raw[n:]
     carried_high, carried_low = halves(padded(err_ref[0, 0], err_ref[0, 1]))
-    of_err = dot_rows(split[: 2 * n], carried_high)
+    of_err = dot_rows(split, carried_high)
     of_err = of_err[:n] + (of_err[n:] + dot_rows(high, carried_low))
     lane = lax.broadcasted_iota(jnp.int32, (1, 128), 1)
     left = lane < HALF
@@ -88,15 +87,20 @@
 
 def right_kernel(
     all_tokens, pay_ref, len_ref, label_ref, grad_ref, act_ref, err_ref,
-    basis_ref, q_ref, raw_ref,
+    basis_ref, q_ref, merged_ref,
 ):
     rank = pay_ref.shape[0] // 2
     hidden = err_ref.shape[2]
     factor = factor_of(pay_ref, all_tokens)
     _, masked = masked_rows(len_ref[...], label_ref[...], grad_ref[...])
-    for part in range(raw_ref.shape[1] // TILE):
+    parts = act_ref.shape[1] // TILE
+    for part in range(parts):
         at = pl.ds(part * TILE, TILE)
-        raw_ref[:, at] = dot(masked, act_ref[:, at]).astype(BF16)
+        raw = dot(masked, act_ref[:, at]).astype(BF16).astype(F32)
+        carried = padded(err_ref[0, 0, :, at], err_ref[0, 1, :, at])
+        high, low = halves(factor * raw + carried)
+        merged_ref[: 2 * HALF, at] = high
+        merged_ref[2 * HALF :, at] = low
     lane = lax.broadcasted_iota(jnp.int32, (1, 128), 1)
     p_sum = factor * pay_ref[:rank] + pay_ref[rank:]
     first = basis_of(jnp.where(lane < hidden, p_sum, 0.0))
@@ -109,11 +113,8 @@
     bottom = jnp.concatenate([low, jnp.zeros_like(low)], axis=1)
     lhs = jnp.concatenate([top, bottom], axis=0)
     width = q_ref.shape[2]
-    for part in range(raw_ref.shape[1] // TILE):
-        at = pl.ds(part * TILE, TILE)
-        carried = padded(err_ref[0, 0, :, at], err_ref[0, 1, :, at])
-        high, low = halves(factor * raw_ref[:, at].astype(F32) + carried)
-        both = dot(lhs, jnp.concatenate([high, low], axis=0))
+    for part in range(parts):
+        both = dot(lhs, merged_ref[:, part * TILE : (part + 1) * TILE])
         q_local = both[: 2 * rank] + both[2 * rank :]
         for block in range(TILE // width):
             q_ref[part * (TILE // width) + block] = q_local[:, block * width : (block + 1) * width]
@@ -201,7 +202,7 @@
             jax.ShapeDtypeStruct((2 * rank, 128), F32),
             jax.ShapeDtypeStruct((outer, 2 * rank, features // outer), F32),
         ],
-        scratch_shapes=[pltpu.VMEM((2 * HALF, features), BF16)],
+        scratch_shapes=[pltpu.VMEM((4 * HALF, features), BF16)],
         compiler_params=pltpu.CompilerParams(vmem_limit_bytes=LIMIT),
         name="right",
     )(payload, lengths, labels, grad, activations, error_state)

time: 96.7 us -> 96.6 us (level)
  no operation moved by 1% of the time
where the time goes in v8:
time: 96.6 us; the launch traced here: 96.3 us
  blocking collectives  88.3 us (91%)
  Pallas kernels  7.08 us (7%)
    all_to_all x5, blocking collectives, exchange(): return lax.all_to_all(blocks, axis, 0, 0, tiled=True)  84.8 us
    pallas_call x1, Pallas kernels, terms(): pl.pallas_call(terms_kernel, grid=(1,), in_specs=[once(x) for x in operan...  3.96 us
    all_gather x1, blocking collectives, local(): payload = lax.all_gather(half, 'core', axis=0, tiled=True)  3.59 us

profile of v8, /device:TPU:1, one launch (start us, length us, event | category | flops | bytes accessed | tf_op | source)
XLA Modules:
  0.0 96.3 jit_solution(9764775938596095057)
XLA Ops:
  0.6 0.0 copy-start
  0.6 0.0 copy-start.1
  0.7 0.0 copy-start.2
  0.7 0.0 copy-start.3
  0.7 0.0 copy-start.4
  0.7 4.0 %terms.1 = f32[16,16,128]{2,1,0:T(8,128)} custom-call(s32[1,8]{1,0:T(1,128)} %len_ref.5, s32[1,128]{1,0:T(1,128)} %bitcast.7, bf16[112,128]{1,0:T(8,128)(2,1)} %bitcast.4, bf16[128,4096]{1,0:T(8,128)(2,1)} %act_ref.5, f32[1,2,56,4096]{3,2,1,0:T(8,128)} %err_ref.5, f32[2,8,4096]{2,1,0:T(8,128)} %warm_ref.1), custom_call_target="tpu_custom_call" | custom-call | tf_op jit(solution)/shard_map/terms/pallas_call | solution.py:184
  4.6 18.2 %all_to_all.25 = f32[32,8,128]{2,1,0:T(8,128)S(1)} all-to-all(f32[32,8,128]{2,1,0:T(8,128)} %bitcast.10), channel_id=1, replica_groups=mesh['replica'=16,'chip'=16,'core'=2] {'chip','core'}, dimensions={0} | all-to-all | bytes 262144 | tf_op jit(solution)/shard_map/all_to_all | solution.py:164
  22.9 24.4 %all_to_all.26 = f32[16,8,128]{2,1,0:T(8,128)S(1)} all-to-all(f32[16,8,128]{2,1,0:T(8,128)S(1)} %broadcast_in_dim.6), channel_id=1, replica_groups=mesh['replica'=16,'chip'=16,'core'=2] {'replica'}, dimensions={0} | all-to-all | bytes 131072 | tf_op jit(solution)/shard_map/all_to_all | solution.py:164
  47.3 3.6 %all_gather.3.pay_ref = f32[16,128]{1,0:T(8,128)S(1)} all-gather(f32[8,128]{1,0:T(8,128)S(1)} %reduce_sum.37), channel_id=1, replica_groups=mesh['replica'=16,'chip'=16,'core'=2] {'core'}, dimensions={0}, use_global_device_ids=true | all-gather | bytes 12288 | tf_op jit(solution)/shard_map/all_gather | solution.py:241
  50.9 0.0 copy-done
  50.9 0.0 copy-done.1
  50.9 0.0 copy-done.2
  50.9 0.0 copy-done.3
  50.9 0.0 copy-done.4
  50.9 1.4 %right.1 = (f32[16,128]{1,0:T(8,128)S(1)}, f32[32,16,128]{2,1,0:T(8,128)S(1)}) custom-call(f32[16,128]{1,0:T(8,128)S(1)} %all_gather.3.pay_ref, s32[1,8]{1,0:T(1,128)S(1)} %copy-done.3, s32[1,128]{1,0:T(1,128)S(1)} %bitcast.8, bf16[112,128]{1,0:T(8,128)(2,1)S(1)} %bitcast.5, bf16[128,4096]{1,0:T(8,128)(2,1)S(1)} %copy-done.1, f32[1,2,56,4096]{3,2,1,0:T(8,128)S(1)} %copy-done), custom_call_target="tpu_custom_call" | custom-call | tf_op jit(solution)/shard_map/right/pallas_call | solution.py:197
  52.3 12.3 %all_to_all.27 = f32[32,16,128]{2,1,0:T(8,128)S(1)} all-to-all(f32[32,16,128]{2,1,0:T(8,128)S(1)} %get-tuple-element.9), channel_id=1, replica_groups=mesh['replica'=16,'chip'=16,'core'=2] {'chip','core'}, dimensions={0} | all-to-all | bytes 524288 | tf_op jit(solution)/shard_map/all_to_all | solution.py:164
  64.7 14.6 %all_to_all.28 = f32[16,16,128]{2,1,0:T(8,128)S(1)} all-to-all(f32[16,16,128]{2,1,0:T(8,128)S(1)} %broadcast_in_dim.7), channel_id=1, replica_groups=mesh['replica'=16,'chip'=16,'core'=2] {'replica'}, dimensions={0} | all-to-all | bytes 262144 | tf_op jit(solution)/shard_map/all_to_all | solution.py:164
  79.4 15.2 %all_to_all.29.sum_ref = f32[32,16,128]{2,1,0:T(8,128)S(1)} all-to-all(f32[32,16,128]{2,1,0:T(8,128)S(1)} %broadcast_in_dim.8), channel_id=1, replica_groups=mesh['replica'=16,'chip'=16,'core'=2] {'chip','core'}, dimensions={0} | all-to-all | bytes 524288 | tf_op jit(solution)/shard_map/all_to_all | solution.py:164
  94.5 1.8 %error.1 = (f32[2,8,56]{2,1,0:T(8,128)}, f32[2,8,4096]{2,1,0:T(8,128)}, f32[1,2,56,4096]{3,2,1,0:T(8,128)}) custom-call(f32[16,128]{1,0:T(8,128)S(1)} %all_gather.3.pay_ref, f32[16,128]{1,0:T(8,128)S(1)} %get-tuple-element.8.basis_ref, f32[32,16,128]{2,1,0:T(8,128)S(1)} %all_to_all.29.sum_ref, s32[1,8]{1,0:T(1,128)S(1)} %copy-done.3, s32[1,128]{1,0:T(1,128)S(1)} %bitcast.9, ...), custom_call_target="tpu_custom_call" | custom-call | tf_op jit(solution)/shard_map/error/pallas_call | solution.py:216
  (7 shorter events, 0.1 us)
Async XLA Ops:
  0.6 50.3 %copy-start = (f32[1,2,56,4096]{3,2,1,0:T(8,128)S(1)}, f32[1,2,56,4096]{3,2,1,0:T(8,128)}, u32[]{:S(2)}) copy-start(f32[1,2,56,4096]{3,2,1,0:T(8,128)} %err_ref.5) | copy-start | bytes 5505028
  0.6 50.3 %copy-start.1 = (bf16[128,4096]{1,0:T(8,128)(2,1)S(1)}, bf16[128,4096]{1,0:T(8,128)(2,1)}, u32[]{:S(2)}) copy-start(bf16[128,4096]{1,0:T(8,128)(2,1)} %act_ref.5) | copy-start | bytes 3145732
  0.7 50.3 %copy-start.2 = (bf16[128,112]{0,1:T(8,128)(2,1)S(1)}, bf16[128,112]{0,1:T(8,128)(2,1)}, u32[]{:S(2)}) copy-start(bf16[128,112]{0,1:T(8,128)(2,1)} %param.7) | copy-start | bytes 86020
  0.7 50.2 %copy-start.3 = (s32[1,8]{1,0:T(1,128)S(1)}, s32[1,8]{1,0:T(1,128)}, u32[]{:S(2)}) copy-start(s32[1,8]{1,0:T(1,128)} %len_ref.5) | copy-start | bytes 100
  0.7 50.2 %copy-start.4 = (s32[128]{0:T(128)S(1)}, s32[128]{0:T(128)}, u32[]{:S(2)}) copy-start(s32[128]{0:T(128)} %param.8) | copy-start | bytes 1540

commit v9 on v8

--- a/solution.py
+++ b/solution.py
@@ -70,15 +70,18 @@
 
 
 def basis_of(vectors):
-    row = lax.broadcasted_iota(jnp.int32, (vectors.shape[0], 1), 0)
-    for r in range(vectors.shape[0]):
-        current = vectors[r : r + 1]
+    rank = vectors.shape[0]
+    row = lax.broadcasted_iota(jnp.int32, (rank, 1), 0)
+    basis = jnp.zeros_like(vectors)
+    for r in range(rank):
+        current = jnp.broadcast_to(vectors[r : r + 1], vectors.shape)
+        own = jnp.sum(current * current, axis=1, keepdims=True)
         dots = jnp.sum(vectors * current, axis=1, keepdims=True)
-        norm = jnp.sqrt(dots[r : r + 1]) + 1e-08
+        norm = jnp.sqrt(own) + 1e-08
         unit = current / norm
-        later = vectors - (dots / norm) * unit
-        vectors = jnp.where(row == r, unit, jnp.where(row > r, later, vectors))
-    return vectors
+        basis = jnp.where(row == r, unit, basis)
+        vectors = vectors - (dots / norm) * unit
+    return basis
 
 
 def factor_of(pay_ref, all_tokens):

time: 96.6 us -> 96.6 us (level)
  no operation moved by 1% of the time
where the time goes in v9:
time: 96.6 us; the launch traced here: 96.3 us
  blocking collectives  88.3 us (91%)
  Pallas kernels  7.07 us (7%)
    all_to_all x5, blocking collectives, exchange(): return lax.all_to_all(blocks, axis, 0, 0, tiled=True)  84.7 us
    pallas_call x1, Pallas kernels, terms(): pl.pallas_call(terms_kernel, grid=(1,), in_specs=[once(x) for x in operan...  3.96 us
    all_gather x1, blocking collectives, local(): payload = lax.all_gather(half, 'core', axis=0, tiled=True)  3.59 us

profile of v9, /device:TPU:1, one launch (start us, length us, event | category | flops | bytes accessed | tf_op | source)
XLA Modules:
  0.0 96.3 jit_solution(5741131705485655572)
XLA Ops:
  0.6 0.0 copy-start
  0.6 0.0 copy-start.1
  0.7 0.0 copy-start.2
  0.7 0.0 copy-start.3
  0.7 0.0 copy-start.4
  0.7 4.0 %terms.1 = f32[16,16,128]{2,1,0:T(8,128)} custom-call(s32[1,8]{1,0:T(1,128)} %len_ref.5, s32[1,128]{1,0:T(1,128)} %bitcast.7, bf16[112,128]{1,0:T(8,128)(2,1)} %bitcast.4, bf16[128,4096]{1,0:T(8,128)(2,1)} %act_ref.5, f32[1,2,56,4096]{3,2,1,0:T(8,128)} %err_ref.5, f32[2,8,4096]{2,1,0:T(8,128)} %warm_ref.1), custom_call_target="tpu_custom_call" | custom-call | tf_op jit(solution)/shard_map/terms/pallas_call | solution.py:187
  4.6 18.2 %all_to_all.25 = f32[32,8,128]{2,1,0:T(8,128)S(1)} all-to-all(f32[32,8,128]{2,1,0:T(8,128)} %bitcast.10), channel_id=1, replica_groups=mesh['replica'=16,'chip'=16,'core'=2] {'chip','core'}, dimensions={0} | all-to-all | bytes 262144 | tf_op jit(solution)/shard_map/all_to_all | solution.py:167
  22.9 24.4 %all_to_all.26 = f32[16,8,128]{2,1,0:T(8,128)S(1)} all-to-all(f32[16,8,128]{2,1,0:T(8,128)S(1)} %broadcast_in_dim.6), channel_id=1, replica_groups=mesh['replica'=16,'chip'=16,'core'=2] {'replica'}, dimensions={0} | all-to-all | bytes 131072 | tf_op jit(solution)/shard_map/all_to_all | solution.py:167
  47.3 3.6 %all_gather.3.pay_ref = f32[16,128]{1,0:T(8,128)S(1)} all-gather(f32[8,128]{1,0:T(8,128)S(1)} %reduce_sum.37), channel_id=1, replica_groups=mesh['replica'=16,'chip'=16,'core'=2] {'core'}, dimensions={0}, use_global_device_ids=true | all-gather | bytes 12288 | tf_op jit(solution)/shard_map/all_gather | solution.py:244
  50.9 0.0 copy-done
  50.9 0.0 copy-done.1
  50.9 0.0 copy-done.2
  50.9 0.0 copy-done.3
  50.9 0.0 copy-done.4
  50.9 1.3 %right.1 = (f32[16,128]{1,0:T(8,128)S(1)}, f32[32,16,128]{2,1,0:T(8,128)S(1)}) custom-call(f32[16,128]{1,0:T(8,128)S(1)} %all_gather.3.pay_ref, s32[1,8]{1,0:T(1,128)S(1)} %copy-done.3, s32[1,128]{1,0:T(1,128)S(1)} %bitcast.8, bf16[112,128]{1,0:T(8,128)(2,1)S(1)} %bitcast.5, bf16[128,4096]{1,0:T(8,128)(2,1)S(1)} %copy-done.1, f32[1,2,56,4096]{3,2,1,0:T(8,128)S(1)} %copy-done), custom_call_target="tpu_custom_call" | custom-call | tf_op jit(solution)/shard_map/right/pallas_call | solution.py:200
  52.3 12.3 %all_to_all.27 = f32[32,16,128]{2,1,0:T(8,128)S(1)} all-to-all(f32[32,16,128]{2,1,0:T(8,128)S(1)} %get-tuple-element.9), channel_id=1, replica_groups=mesh['replica'=16,'chip'=16,'core'=2] {'chip','core'}, dimensions={0} | all-to-all | bytes 524288 | tf_op jit(solution)/shard_map/all_to_all | solution.py:167
  64.7 14.6 %all_to_all.28 = f32[16,16,128]{2,1,0:T(8,128)S(1)} all-to-all(f32[16,16,128]{2,1,0:T(8,128)S(1)} %broadcast_in_dim.7), channel_id=1, replica_groups=mesh['replica'=16,'chip'=16,'core'=2] {'replica'}, dimensions={0} | all-to-all | bytes 262144 | tf_op jit(solution)/shard_map/all_to_all | solution.py:167
  79.4 15.2 %all_to_all.29.sum_ref = f32[32,16,128]{2,1,0:T(8,128)S(1)} all-to-all(f32[32,16,128]{2,1,0:T(8,128)S(1)} %broadcast_in_dim.8), channel_id=1, replica_groups=mesh['replica'=16,'chip'=16,'core'=2] {'chip','core'}, dimensions={0} | all-to-all | bytes 524288 | tf_op jit(solution)/shard_map/all_to_all | solution.py:167
  94.5 1.8 %error.1 = (f32[2,8,56]{2,1,0:T(8,128)}, f32[2,8,4096]{2,1,0:T(8,128)}, f32[1,2,56,4096]{3,2,1,0:T(8,128)}) custom-call(f32[16,128]{1,0:T(8,128)S(1)} %all_gather.3.pay_ref, f32[16,128]{1,0:T(8,128)S(1)} %get-tuple-element.8.basis_ref, f32[32,16,128]{2,1,0:T(8,128)S(1)} %all_to_all.29.sum_ref, s32[1,8]{1,0:T(1,128)S(1)} %copy-done.3, s32[1,128]{1,0:T(1,128)S(1)} %bitcast.9, ...), custom_call_target="tpu_custom_call" | custom-call | tf_op jit(solution)/shard_map/error/pallas_call | solution.py:219
  (7 shorter events, 0.1 us)
Async XLA Ops:
  0.6 50.3 %copy-start = (f32[1,2,56,4096]{3,2,1,0:T(8,128)S(1)}, f32[1,2,56,4096]{3,2,1,0:T(8,128)}, u32[]{:S(2)}) copy-start(f32[1,2,56,4096]{3,2,1,0:T(8,128)} %err_ref.5) | copy-start | bytes 5505028
  0.6 50.3 %copy-start.1 = (bf16[128,4096]{1,0:T(8,128)(2,1)S(1)}, bf16[128,4096]{1,0:T(8,128)(2,1)}, u32[]{:S(2)}) copy-start(bf16[128,4096]{1,0:T(8,128)(2,1)} %act_ref.5) | copy-start | bytes 3145732
  0.7 50.3 %copy-start.2 = (bf16[128,112]{0,1:T(8,128)(2,1)S(1)}, bf16[128,112]{0,1:T(8,128)(2,1)}, u32[]{:S(2)}) copy-start(bf16[128,112]{0,1:T(8,128)(2,1)} %param.7) | copy-start | bytes 86020
  0.7 50.2 %copy-start.3 = (s32[1,8]{1,0:T(1,128)S(1)}, s32[1,8]{1,0:T(1,128)}, u32[]{:S(2)}) copy-start(s32[1,8]{1,0:T(1,128)} %len_ref.5) | copy-start | bytes 100
  0.7 50.2 %copy-start.4 = (s32[128]{0:T(128)S(1)}, s32[128]{0:T(128)}, u32[]{:S(2)}) copy-start(s32[128]{0:T(128)} %param.8) | copy-start | bytes 1540
